TPU v7x, 512 devices: a whole 4x4x16 slice. The times are simulated.
512 devices in a mesh: dp: 8 (over x, core), seq: 64 (over y, z).
Axes of the slice: x: 4, y: 4, z: 16, core: 2. Of those that a mesh axis runs over, the one named last changes fastest.
Arguments:
- inputs: bfloat16 [8, 128, 128, 1152], P('dp', 'seq'), may hold values from -6 to 6
- mid_inputs: bfloat16 [8, 128, 128, 1152], P('dp', 'seq'), may hold values from -6 to 6
- cotangent: bfloat16 [8, 128, 128, 1152], P('dp', 'seq'), may hold values from -6 to 6
- modulation: float32 [8, 6, 1152], P('dp'), may hold values from -4 to 4
- valid_frames: int32 [8], P('dp'), may hold values from 64 to 128, as said below
- qkv_spatial: bfloat16 [1152, 1728], P('dp', 'seq'), may hold values from -1 to 1
- out_spatial: bfloat16 [576, 1152], P('dp', 'seq'), may hold values from -0.25 to 0.25
- qkv_temporal: bfloat16 [1152, 1728], P('dp', 'seq'), may hold values from -1 to 1
- out_temporal: bfloat16 [576, 1152], P('dp', 'seq'), may hold values from -0.25 to 0.25
Outputs:
- input_grad: bfloat16 [8, 128, 128, 1152], P('dp', 'seq')
Inputs may be any that keep to these rules, and one draw needn't show every extreme that they name: `valid_frames`: frames from a clip's count on are padding; one clip has all 128 frames valid and another exactly 64.
All inputs are finite; a program needn't handle non-finite values.
Results may differ from a plain program's by a relative error of at most 0.024.
The roundings to bfloat16 on the way count: a program that leaves them out, or rounds other values in their place, can miss the bound.
Values may be sent and summed in bfloat16 or wider, within the bound.
A program may use at most 64 MiB of HBM per device.

v0:
```python
import jax
import jax.numpy as jnp
from jax import lax
from jax.sharding import PartitionSpec as P

HDIM = 72


eps = 1e-06


def layer_norm(tokens):
    values = tokens.astype(jnp.float32)
    center = jnp.mean(values, -1, keepdims=True)
    spread = jnp.mean((values - center) ** 2, -1, keepdims=True)
    rstd = lax.rsqrt(spread + eps)
    return ((values - center) * rstd, rstd)


def norm_back(dnorm, normed, rstd, scale):
    grad_n = dnorm.astype(jnp.float32) * (1.0 + scale)
    inner = (
        grad_n
        - jnp.mean(grad_n, -1, keepdims=True)
        - normed * jnp.mean(grad_n * normed, -1, keepdims=True)
    )
    return rstd * inner


def project(tokens, weight):
    return jnp.dot(tokens, weight, preferred_element_type=jnp.float32)


def project_back(tokens, weight):
    dims = (((tokens.ndim - 1,), (1,)), ((), ()))
    return lax.dot_general(tokens, weight, dims, preferred_element_type=jnp.float32)


def attention_grad(qkv, dout, key_live, seq_first):
    width = dout.shape[-1]
    heads = width // HDIM
    scale = HDIM ** (-0.5)
    lead = qkv.shape[:-1]
    query = qkv[..., :width].reshape(lead + (heads, HDIM))
    key_part = qkv[..., width : 2 * width].reshape(lead + (heads, HDIM))
    value = qkv[..., 2 * width :].reshape(lead + (heads, HDIM))
    upstream = dout.reshape(lead + (heads, HDIM))
    if seq_first:
        score_form = "qbhd,kbhd->bhqk"
        value_form = "bhqk,qbhd->kbhd"
        query_form = "bhqk,kbhd->qbhd"
    else:
        score_form = "bqhd,bkhd->bhqk"
        value_form = "bhqk,bqhd->bkhd"
        query_form = "bhqk,bkhd->bqhd"
    scores = jnp.einsum(score_form, query, key_part, preferred_element_type=jnp.float32) * scale
    if key_live is not None:
        scores = jnp.where(key_live, scores, -1e30)
    peak = jnp.max(scores, -1, keepdims=True)
    probs = jnp.exp(scores - peak)
    probs = probs / jnp.sum(probs, -1, keepdims=True)
    probs_b = probs.astype(jnp.bfloat16)
    dvalue = jnp.einsum(value_form, probs_b, upstream, preferred_element_type=jnp.float32)
    dprobs = jnp.einsum(score_form, upstream, value, preferred_element_type=jnp.float32)
    delta = jnp.sum(probs * dprobs, -1, keepdims=True)
    dscore = (probs * (dprobs - delta)).astype(jnp.bfloat16)
    dquery = jnp.einsum(query_form, dscore, key_part, preferred_element_type=jnp.float32) * scale
    dkey = jnp.einsum(value_form, dscore, query, preferred_element_type=jnp.float32) * scale
    parts = [part.reshape(lead + (width,)) for part in (dquery, dkey, dvalue)]
    return jnp.concatenate(parts, -1).astype(jnp.bfloat16)


def per_device(
    inputs,
    mid_inputs,
    cotangent,
    modulation,
    valid_frames,
    qkv_spatial,
    out_spatial,
    qkv_temporal,
    out_temporal,
):
    pieces = (
        lax.all_gather(qkv_spatial, "dp", axis=0, tiled=True),
        lax.all_gather(out_spatial, "dp", axis=0, tiled=True),
        lax.all_gather(qkv_temporal, "dp", axis=0, tiled=True),
        lax.all_gather(out_temporal, "dp", axis=0, tiled=True),
    )
    whole = (
        lax.all_gather(pieces[0], "seq", axis=1, tiled=True),
        lax.all_gather(pieces[1], "seq", axis=1, tiled=True),
        lax.all_gather(pieces[2], "seq", axis=1, tiled=True),
        lax.all_gather(pieces[3], "seq", axis=1, tiled=True),
    )
    spatial_qkv, spatial_out, temporal_qkv, temporal_out = whole
    shifts = modulation[0]
    frame_count = valid_frames[0]
    frames_dev = inputs.shape[1]
    first_frame = lax.axis_index("seq") * frames_dev
    live_frames = first_frame + jnp.arange(frames_dev, dtype=jnp.int32) < frame_count
    masked = jnp.where(live_frames[:, None, None], cotangent[0].astype(jnp.float32), 0.0)
    normed, rstd = layer_norm(mid_inputs[0])
    normin = (normed * (1.0 + shifts[4]) + shifts[3]).astype(jnp.bfloat16)
    gated = (masked * shifts[5]).astype(jnp.bfloat16)
    qkv = project(normin, temporal_qkv).astype(jnp.bfloat16)
    dout = project_back(gated, temporal_out).astype(jnp.bfloat16)
    qkv_patch, dout_patch = (
        lax.all_to_all(qkv, "seq", split_axis=1, concat_axis=0, tiled=True),
        lax.all_to_all(dout, "seq", split_axis=1, concat_axis=0, tiled=True),
    )
    key_live = jnp.arange(qkv_patch.shape[0], dtype=jnp.int32) < frame_count
    dqkv_patch = attention_grad(qkv_patch, dout_patch, key_live, True)
    dqkv = lax.all_to_all(dqkv_patch, "seq", split_axis=0, concat_axis=1, tiled=True)
    dnorm = project_back(dqkv, temporal_qkv).astype(jnp.bfloat16)
    dmid = masked + norm_back(dnorm, normed, rstd, shifts[4])
    normed_s, rstd_s = layer_norm(inputs[0])
    normin_s = (normed_s * (1.0 + shifts[1]) + shifts[0]).astype(jnp.bfloat16)
    qkv_s = project(normin_s, spatial_qkv).astype(jnp.bfloat16)
    gated_s = (dmid * shifts[2]).astype(jnp.bfloat16)
    dout_s = project_back(gated_s, spatial_out).astype(jnp.bfloat16)
    dqkv_s = attention_grad(qkv_s, dout_s, None, False)
    dnorm_s = project_back(dqkv_s, spatial_qkv).astype(jnp.bfloat16)
    result = dmid + norm_back(dnorm_s, normed_s, rstd_s, shifts[1])
    return result.astype(jnp.bfloat16)[None]


def solution(mesh):
    in_specs = (
        P("dp", "seq", None, None),
        P("dp", "seq", None, None),
        P("dp", "seq", None, None),
        P("dp", None, None),
        P("dp"),
        P("dp", "seq"),
        P("dp", "seq"),
        P("dp", "seq"),
        P("dp", "seq"),
    )
    out_specs = P("dp", "seq", None, None)
    return jax.shard_map(
        per_device, mesh=mesh, in_specs=in_specs, out_specs=out_specs, check_vma=False
    )
```

profile of v0, /device:TPU:1, one launch (start us, length us, event | category | flops | bytes accessed | tf_op | source)
XLA Modules:
  0.0 641.4 jit_solution(15078359766172086792)
XLA Ops:
  6.5 19.8 %all-gather.2 = bf16[8,72,18]{1,2,0:T(8,128)(2,1)S(1)} all-gather(bf16[1,72,18]{1,2,0:T(8,128)(2,1)} %bitcast.210), channel_id=1, replica_groups=mesh['dp'=8,'seq'=64] {'dp'}, dimensions={0}, use_global_device_ids=true | all-gather | bytes 23328 | tf_op jit(solution)/shard_map/all_gather | solution.py:88
  27.2 13.0 %all-gather = bf16[8,144,27]{1,2,0:T(8,128)(2,1)S(1)} all-gather(bf16[1,144,27]{1,2,0:T(8,128)(2,1)} %bitcast.208), channel_id=1, replica_groups=mesh['dp'=8,'seq'=64] {'dp'}, dimensions={0}, use_global_device_ids=true | all-gather | bytes 69984 | tf_op jit(solution)/shard_map/all_gather | solution.py:87
  41.1 13.0 %all-gather.6 = bf16[8,72,18]{1,2,0:T(8,128)(2,1)S(1)} all-gather(bf16[1,72,18]{1,2,0:T(8,128)(2,1)} %bitcast.211), channel_id=1, replica_groups=mesh['dp'=8,'seq'=64] {'dp'}, dimensions={0}, use_global_device_ids=true | all-gather | bytes 23328 | tf_op jit(solution)/shard_map/all_gather | solution.py:86
  56.2 101.2 %all-gather.15.cloned.1.call-done = bf16[64,18,576]{2,1,0:T(8,128)(2,1)} async-done(((bf16[1,18,576]{2,1,0:T(8,128)(2,1)}), bf16[64,18,576]{2,1,0:T(8,128)(2,1)}) %all-gather.15.cloned.1.call-update) | async-done | bytes 1327120 | tf_op jit(solution)/shard_map/all_gather | solution.py:94
  157.4 2.8 reshape.138
  162.2 9.1 %all-to-all-start.1 = ((bf16[2,128,576]{2,0,1:T(2,128)(2,1)}), bf16[2,128,576]{2,0,1:T(2,128)(2,1)S(1)}, u32[]{:S(2)}, u32[]{:S(2)}) async-start(bf16[2,128,576]{2,0,1:T(2,128)(2,1)} %copy.51), calls=%async_computation.1 | async-start | bytes 655360 | tf_op jit(solution)/shard_map/all_to_all | solution.py:110
  171.8 133.5 %all-gather.13.cloned.1.call-done = bf16[64,27,1152]{2,1,0:T(8,128)(2,1)} async-done(((bf16[1,27,1152]{2,1,0:T(8,128)(2,1)}), bf16[64,27,1152]{2,1,0:T(8,128)(2,1)}) %all-gather.13.cloned.1.call-update) | async-done | bytes 3981328 | tf_op jit(solution)/shard_map/all_gather | solution.py:93
  305.3 7.2 %reshape.147 = bf16[1728,1152,1]{1,0,2:T(8,128)(2,1)} reshape(bf16[64,27,1152]{2,1,0:T(8,128)(2,1)} %all-gather.13.cloned.1.call-done) | data formatting | bytes 7962624
  312.5 3.6 convolution_convert_fusion.1
  316.1 2.2 copy.45
  318.3 9.8 %all-to-all-start = ((bf16[2,128,1728]{2,0,1:T(2,128)(2,1)}), bf16[2,128,1728]{2,0,1:T(2,128)(2,1)S(1)}, u32[]{:S(2)}, u32[]{:S(2)}) async-start(bf16[2,128,1728]{2,0,1:T(2,128)(2,1)} %copy.45), calls=%async_computation | async-start | bytes 1835008 | tf_op jit(solution)/shard_map/all_to_all | solution.py:109
  328.1 21.2 %all-gather.4 = bf16[8,144,27]{1,2,0:T(8,128)(2,1)S(1)} all-gather(bf16[1,144,27]{1,2,0:T(8,128)(2,1)S(1)} %bitcast.209), channel_id=1, replica_groups=mesh['dp'=8,'seq'=64] {'dp'}, dimensions={0}, use_global_device_ids=true | all-gather | bytes 69984 | tf_op jit(solution)/shard_map/all_gather | solution.py:85
  351.6 16.0 %all-to-all-done = bf16[2,128,1728]{2,0,1:T(2,128)(2,1)S(1)} async-done(((bf16[2,128,1728]{2,0,1:T(2,128)(2,1)}), bf16[2,128,1728]{2,0,1:T(2,128)(2,1)S(1)}, u32[]{:S(2)}, u32[]{:S(2)}) %all-to-all-start) | async-done | bytes 884768 | tf_op jit(solution)/shard_map/all_to_all | solution.py:109
  376.7 4.3 concatenate.8
  380.9 12.3 %all-to-all-start.2 = ((bf16[128,2,1728]{2,1,0:T(2,128)(2,1)}), bf16[128,2,1728]{2,1,0:T(2,128)(2,1)S(1)}, u32[]{:S(2)}, u32[]{:S(2)}) async-start(bf16[128,2,1728]{2,1,0:T(2,128)(2,1)} %concatenate.8), calls=%async_computation.2 | async-start | bytes 1835008 | tf_op jit(solution)/shard_map/all_to_all | solution.py:114
  393.7 66.1 %all-gather.19.cloned.1.call-done = bf16[64,18,576]{2,1,0:T(8,128)(2,1)} async-done(((bf16[1,18,576]{2,1,0:T(8,128)(2,1)}), bf16[64,18,576]{2,1,0:T(8,128)(2,1)}) %all-gather.19.cloned.1.call-update) | async-done | bytes 1327120 | tf_op jit(solution)/shard_map/all_gather | solution.py:92
  459.9 3.8 reshape.146
  463.7 141.0 %all-gather.17.cloned.1.call-done = bf16[64,27,1152]{2,1,0:T(8,128)(2,1)} async-done(((bf16[1,27,1152]{2,1,0:T(8,128)(2,1)}), bf16[64,27,1152]{2,1,0:T(8,128)(2,1)}) %all-gather.17.cloned.1.call-update) | async-done | bytes 3981328 | tf_op jit(solution)/shard_map/all_gather | solution.py:91
  604.6 7.2 %reshape.149 = bf16[1728,1152,1]{1,0,2:T(8,128)(2,1)} reshape(bf16[64,27,1152]{2,1,0:T(8,128)(2,1)} %all-gather.17.cloned.1.call-done) | data formatting | bytes 7962624
  611.8 3.6 convolution_convert_fusion
  618.5 3.7 fusion.88
  626.6 2.5 convolution_convert_fusion.4
  629.1 4.0 fusion.87
  633.2 1.6 fusion.61
  (111 shorter events, 24.7 us)
Async XLA Ops:
  6.5 49.0 %copy-start.7 = (f32[1,6,1152]{2,0,1:T(1,128)S(1)}, f32[1,6,1152]{2,0,1:T(1,128)}, u32[]{:S(2)}) copy-start(f32[1,6,1152]{2,0,1:T(1,128)} %param.12) | copy-start | bytes 82948
  6.5 150.8 %all-gather.15.cloned.1.call-start = ((), (), s32[]{:S(2)}) async-start(), calls=%async_computation.4 | async-start | bytes 1996800 | tf_op jit(solution)/shard_map/all_gather | solution.py:94
  27.1 278.2 %all-gather.13.cloned.1.call-start = ((), (), s32[]{:S(2)}) async-start(), calls=%async_computation.3 | async-start | bytes 4792320 | tf_op jit(solution)/shard_map/all_gather | solution.py:93
  41.0 418.8 %all-gather.19.cloned.1.call-start = ((), (), s32[]{:S(2)}) async-start(), calls=%async_computation.6 | async-start | bytes 1996800 | tf_op jit(solution)/shard_map/all_gather | solution.py:92
  55.5 104.6 %copy-start.22 = (pred[2]{0:T(512)(128)(4,1)}, pred[2]{0:T(512)(128)(4,1)S(1)}, u32[]{:S(2)}) copy-start(pred[2]{0:T(512)(128)(4,1)S(1)} %add_compare_fusion) | copy-start | bytes 10
  56.2 256.3 %copy-start.11 = (f32[1152]{0:T(1024)}, f32[1152]{0:T(1024)S(1)}, u32[]{:S(2)}) copy-start(f32[1152]{0:T(1024)S(1)} %get-tuple-element.12) | copy-start | bytes 13828
  56.2 555.6 %copy-start.9 = (f32[1152]{0:T(1024)}, f32[1152]{0:T(1024)S(1)}, u32[]{:S(2)}) copy-start(f32[1152]{0:T(1024)S(1)} %get-tuple-element.9) | copy-start | bytes 13828
  56.2 104.0 %copy-start.4 = (bf16[1,2,128,1152]{3,2,1,0:T(8,128)(2,1)S(1)}, bf16[1,2,128,1152]{3,2,1,0:T(8,128)(2,1)}, u32[]{:S(2)}) copy-start(bf16[1,2,128,1152]{3,2,1,0:T(8,128)(2,1)} %param.11) | copy-start | bytes 1769476
  160.9 10.4 %copy-start.1 = (bf16[1,2,128,1152]{3,2,1,0:T(8,128)(2,1)S(1)}, bf16[1,2,128,1152]{3,2,1,0:T(8,128)(2,1)}, u32[]{:S(2)}) copy-start(bf16[1,2,128,1152]{3,2,1,0:T(8,128)(2,1)} %param.10) | copy-start | bytes 1769476
  162.2 156.1 %all-to-all-start.1 = ((bf16[2,128,576]{2,0,1:T(2,128)(2,1)}), bf16[2,128,576]{2,0,1:T(2,128)(2,1)S(1)}, u32[]{:S(2)}, u32[]{:S(2)}) async-start(bf16[2,128,576]{2,0,1:T(2,128)(2,1)} %copy.51), calls=%async_computation.1 | async-start | bytes 655360 | tf_op jit(solution)/shard_map/all_to_all | solution.py:110
  171.8 140.7 %copy-start.13 = (f32[2,128]{1,0:T(2,128)}, f32[2,128]{1,0:T(2,128)S(1)}, u32[]{:S(2)}) copy-start(f32[2,128]{1,0:T(2,128)S(1)} %add_rsqrt_fusion.1) | copy-start | bytes 3076
  318.2 9.8 %copy-start.8 = (bf16[144,27]{0,1:T(8,128)(2,1)S(1)}, bf16[144,27]{0,1:T(8,128)(2,1)}, u32[]{:S(2)}) copy-start(bf16[144,27]{0,1:T(8,128)(2,1)} %param.14) | copy-start | bytes 23332
  318.3 49.3 %all-to-all-start = ((bf16[2,128,1728]{2,0,1:T(2,128)(2,1)}), bf16[2,128,1728]{2,0,1:T(2,128)(2,1)S(1)}, u32[]{:S(2)}, u32[]{:S(2)}) async-start(bf16[2,128,1728]{2,0,1:T(2,128)(2,1)} %copy.45), calls=%async_computation | async-start | bytes 1835008 | tf_op jit(solution)/shard_map/all_to_all | solution.py:109
  328.0 276.6 %all-gather.17.cloned.1.call-start = ((), (), s32[]{:S(2)}) async-start(), calls=%async_computation.5 | async-start | bytes 4792320 | tf_op jit(solution)/shard_map/all_gather | solution.py:91
  380.9 12.3 %copy-start = (bf16[1,2,128,1152]{3,2,1,0:T(8,128)(2,1)S(1)}, bf16[1,2,128,1152]{3,2,1,0:T(8,128)(2,1)}, u32[]{:S(2)}) copy-start(bf16[1,2,128,1152]{3,2,1,0:T(8,128)(2,1)} %param.9) | copy-start | bytes 1769476
  380.9 236.8 %all-to-all-start.2 = ((bf16[128,2,1728]{2,1,0:T(2,128)(2,1)}), bf16[128,2,1728]{2,1,0:T(2,128)(2,1)S(1)}, u32[]{:S(2)}, u32[]{:S(2)}) async-start(bf16[128,2,1728]{2,1,0:T(2,128)(2,1)} %concatenate.8), calls=%async_computation.2 | async-start | bytes 1835008 | tf_op jit(solution)/shard_map/all_to_all | solution.py:114
  393.7 218.1 %copy-start.16 = (f32[2,128]{1,0:T(2,128)}, f32[2,128]{1,0:T(2,128)S(1)}, u32[]{:S(2)}) copy-start(f32[2,128]{1,0:T(2,128)S(1)} %add_rsqrt_fusion) | copy-start | bytes 3076
  618.5 3.8 copy-start.2
  618.5 3.8 copy-start.5
  629.1 4.1 copy-start.15
  629.1 4.1 copy-start.17
  629.1 4.1 copy-start.19
  629.1 4.1 copy-start.21
  629.1 4.1 copy-start.24
  (9 other events, 14.7 us)
Sparse Core Ops, SparseCore 0:
  27.2 130.0 all-gather.14
  160.3 144.9 all-gather.12
  308.2 151.5 all-gather.18
  462.7 141.9 all-gather.16
where the time goes:
time: 649 us; the launch traced here: 641 us
  waiting for transfers between devices  458 us (71%)
  blocking collectives  67 us (10%)
  local copies, waits for them, and re-layouts  41.4 us (6%)
  starting transfers between devices  31.3 us (5%)
  matrix products  25.9 us (4%)
  between operations  14.3 us (2%)
    all_gather x1, waiting for transfers between devices, per_device(): lax.all_gather(pieces[0], 'seq', axis=1, tiled=True)  141 us
    all_gather x1, waiting for transfers between devices, per_device(): lax.all_gather(pieces[2], 'seq', axis=1, tiled=True)  133 us
    all_gather x1, waiting for transfers between devices, per_device(): lax.all_gather(pieces[3], 'seq', axis=1, tiled=True)  101 us
    all_gather x1, waiting for transfers between devices, per_device(): lax.all_gather(pieces[1], 'seq', axis=1, tiled=True)  66.1 us
    unnamed x60, local copies, waits for them, and re-layouts  24.4 us
    all_gather x1, blocking collectives, per_device(): lax.all_gather(qkv_spatial, 'dp', axis=0, tiled=True)  21.2 us
    all_gather x1, blocking collectives, per_device(): lax.all_gather(out_temporal, 'dp', axis=0, tiled=True)  19.8 us
    all_to_all x1, waiting for transfers between devices, per_device(): lax.all_to_all(qkv, 'seq', split_axis=1, concat_axis=0, tiled=True)  16 us
  transfers between devices with their start and end apart: 7, of which 5 were waited for; matrix products, arithmetic and copies ran while one was open for 8% of the time, Pallas kernels for 0%

commit v1 on v0

v1 whole, which is shorter than its diff:
```python
import jax
import jax.numpy as jnp
from jax import lax
from jax.experimental import pallas as pl
from jax.experimental.pallas import tpu as pltpu
from jax.sharding import PartitionSpec as P

HDIM = 72
HEADS = 8
D = 1152
EPS = 1e-06
TOK = 256
NY, NX, NZ = 4, 4, 16
NSEQ = NY * NZ
QW = 512
OW = 384
HP = 80
f32, bf16 = jnp.float32, jnp.bfloat16

NN = (((1,), (0,)), ((), ()))
NT = (((1,), (1,)), ((), ()))
TN = (((0,), (0,)), ((), ()))


def dot(a, b, dims=NN):
    return lax.dot_general(a, b, dims, preferred_element_type=f32)


def iota(shape, axis):
    return lax.broadcasted_iota(jnp.int32, shape, axis)


def head_at(n):
    return (n // 6) * QW + (n % 6) * HDIM


def norm_stats(x):
    center = jnp.mean(x, -1, keepdims=True)
    diff = x - center
    spread = jnp.mean(diff * diff, -1, keepdims=True)
    rstd = lax.rsqrt(spread + EPS)
    return diff * rstd, rstd


def norm_back(dnorm, normed, rstd, gain):
    g = dnorm * gain
    return rstd * (
        g
        - jnp.mean(g, -1, keepdims=True)
        - normed * jnp.mean(g * normed, -1, keepdims=True)
    )


def kernel(
    inp, mid, cot, mod, frames, qkv_s, out_s, qkv_t, out_t, result,
    zbuf, eq, eo, q_t, o_t, q_s, o_s,
    msend, mrecv, dsend, drecv, rsend, rrecv,
    pm, pr, normin, qkv, dqkv, dout, probs, acc, nm_t, rs_t, nm_s, rs_s, dmid,
    zsend_sem, zrecv_sem, jsend_sem, jrecv_sem, asend_sem, arecv_sem,
):
    dp = lax.axis_index("dp")
    s = lax.axis_index("seq")
    x, c = dp // 2, dp % 2
    y, z = s // NZ, s % NZ
    other = 1 - c
    pending = []

    def seq_dev(yy, zz):
        return {"seq": yy * NZ + zz}

    def x_dev(xx):
        return {"dp": xx * 2 + c}

    def peer(j):
        t = j // 4
        dz = jnp.where(t % 2 == 1, (t + 1) // 2, NZ - t // 2)
        return ((y + j % 4) % NY) * NZ + (z + dz) % NZ

    barrier = pltpu.get_barrier_semaphore()

    def greet(j, carry):
        pl.semaphore_signal(barrier, inc=1, device_id={"seq": peer(j)})
        return carry

    for xx in ((x + 1) % NX, (x + 3) % NX):
        pl.semaphore_signal(barrier, inc=1, device_id=x_dev(xx))
    pl.semaphore_signal(barrier, inc=1, device_id={"dp": x * 2 + other})
    lax.fori_loop(1, NSEQ, greet, 0)

    def pack(qkv_ref, out_ref):
        q, o = qkv_ref[...], out_ref[...]

        def place(rows, g):
            hit = iota((rows, 128), 1) == iota((rows, 128), 0) + 32 * g
            return jnp.where(hit, 1.0, 0.0).astype(bf16)

        q0 = dot(q, place(27, 0), TN)[0:64]
        q1 = dot(q, place(27, 1), TN)[64:128]
        q2 = dot(q, place(27, 2), TN)[128:144]
        o2 = dot(o, place(18, 2))[0:48]
        o3 = dot(o, place(18, 3))[48:72]
        full = q0 + q1 + jnp.concatenate([q2, o2], 0)
        full = full + jnp.concatenate([o3, jnp.zeros((40, 128), f32)], 0)
        return full.astype(bf16)

    zbuf[z, 0:64] = pack(qkv_t, out_t)
    zbuf[z, 64:128] = pack(qkv_s, out_s)

    ri, ci = iota((TOK, TOK), 0), iota((TOK, TOK), 1)
    pm[...] = jnp.where(ci == (ri & 1) * 128 + (ri >> 2) * 2 + ((ri >> 1) & 1), 1.0, 0.0).astype(bf16)
    pr[...] = jnp.where(
        ci == ((ri & 127) >> 1) * 4 + (ri >> 7) * 2 + (ri & 1), 1.0, 0.0
    ).astype(bf16)

    msend[...] = dot(pm[...], mid[...].reshape(TOK, D)).astype(bf16).reshape(NSEQ, 4, D)

    pl.semaphore_wait(barrier, NSEQ - 1 + 3)

    def zcopy(block, way, step):
        to = (z + 1) % NZ if way == 0 else (z + NZ - 1) % NZ
        return pltpu.make_async_remote_copy(
            src_ref=zbuf.at[block], dst_ref=zbuf.at[block],
            send_sem=zsend_sem.at[way, step], recv_sem=zrecv_sem.at[way, step],
            device_id=seq_dev(y, to),
        )

    def scatter(src, dst, k, lo, hi):
        def one(j, carry):
            to = peer(j)
            pltpu.make_async_remote_copy(
                src_ref=src.at[to], dst_ref=dst.at[s],
                send_sem=asend_sem.at[k], recv_sem=arecv_sem.at[k],
                device_id={"seq": to},
            ).start()
            return carry
        lax.fori_loop(lo, hi, one, 0)

    def wait_scatter(ref, sem, k):
        part = ref.at[pl.ds(0, NSEQ - 1)]
        pltpu.make_async_copy(part, part, sem.at[k]).wait()

    for step in range(8):
        if step > 0:
            zcopy((z + NZ - step) % NZ, 0, step - 1).wait_recv()
        cp = zcopy((z + NZ - step) % NZ, 0, step)
        cp.start()
        pending.append(cp)
        if step > 0:
            zcopy((z + step) % NZ, 1, step - 1).wait_recv()
        if step < 7:
            cp = zcopy((z + step) % NZ, 1, step)
            cp.start()
            pending.append(cp)
            scatter(msend, mrecv, 0, 1 + 9 * step, 10 + 9 * step)
        if step == 0:
            def fill(zz, carry):
                lane = iota((224, QW), 0) - 96
                live = (lane >= 0) & (lane < 27)
                hit = live & (iota((224, QW), 1) == lane + 27 * zz)
                eq[zz] = jnp.where(hit, 1.0, 0.0).astype(bf16)
                lane = iota((224, OW), 0) - 96
                live = (lane >= 0) & (lane < 18)
                hit = live & (iota((224, OW), 1) == lane + 18 * zz + 32 * y)
                eo[zz] = jnp.where(hit, 1.0, 0.0).astype(bf16)
                return carry
            lax.fori_loop(0, NZ, fill, 0)
    zcopy((z + NZ - 8) % NZ, 0, 7).wait_recv()

    def unpack(at, q_ref, o_ref):
        whole = jnp.concatenate([zbuf[i, at:at + 64] for i in range(NZ)], 1)

        def pick(table, g):
            lo = 96 - 32 * g
            return dot(whole, table[:, lo:lo + 128, :].reshape(NZ * 128, -1)).astype(bf16)

        o_ref[y, c, x] = jnp.concatenate([pick(eo, 2)[16:64], pick(eo, 3)[0:32]], 0)
        q_ref[y, c, x] = jnp.concatenate([pick(eq, 0), pick(eq, 1), pick(eq, 2)[0:16]], 0)

    jobs_t = [
        (0, o_t, "y", 0, 48, 32), (1, o_t, "x", 48, 32, 16),
        (2, q_t, "y", 0, 80, 48), (3, q_t, "x", 80, 64, 32),
    ]
    jobs_s = [
        (4, o_s, "y", 0, 48, 32), (5, o_s, "x", 48, 32, 16),
        (6, q_s, "y", 0, 80, 48), (7, q_s, "x", 80, 64, 32),
    ]

    def view(job, phase, rel, half, core):
        _, ref, first, r, n, m = job
        lo, size = {"all": (r, n), "a": (r, m), "b": (r + m, n - m)}[half]
        rows = pl.ds(lo, size)
        axis = first if phase == 0 else ("x" if first == "y" else "y")
        if axis == "x":
            return ref.at[y if phase == 0 else slice(None), core, (x + rel) % NX, rows]
        return ref.at[(y + rel) % NY, core, x if phase == 0 else slice(None), rows]

    def hop(job, phase, rel, half, way, slot):
        first = job[2]
        axis = first if phase == 0 else ("x" if first == "y" else "y")
        step = 1 if way == 0 else 3
        dev = x_dev((x + step) % NX) if axis == "x" else seq_dev((y + step) % NY, z)
        ref = view(job, phase, rel, half, c)
        return pltpu.make_async_remote_copy(
            src_ref=ref, dst_ref=ref,
            send_sem=jsend_sem.at[job[0], phase * 4 + slot],
            recv_sem=jrecv_sem.at[job[0], phase * 4 + slot],
            device_id=dev,
        )

    def go(cp):
        cp.start()
        pending.append(cp)

    def first_step(job, phase):
        go(hop(job, phase, 0, "all", 0, 0))
        go(hop(job, phase, 0, "all", 1, 1))

    def pass_on(job, phase):
        hop(job, phase, 3, "all", 0, 0).wait_recv()
        go(hop(job, phase, 3, "a", 0, 2))
        hop(job, phase, 1, "all", 1, 1).wait_recv()
        go(hop(job, phase, 1, "b", 1, 3))

    def last_step(job, phase):
        hop(job, phase, 2, "a", 0, 2).wait_recv()
        hop(job, phase, 2, "b", 1, 3).wait_recv()

    def share(job, rel, core):
        ref = view(job, 1, rel, "all", core)
        return pltpu.make_async_remote_copy(
            src_ref=ref, dst_ref=ref,
            send_sem=jsend_sem.at[job[0], 8 + rel], recv_sem=jrecv_sem.at[job[0], 8 + rel],
            device_id={"dp": x * 2 + other},
        )

    def share_wait(job):
        for rel in range(4):
            share(job, rel, other).wait_recv()

    unpack(0, q_t, o_t)
    for job in jobs_t:
        first_step(job, 0)
    unpack(64, q_s, o_s)
    for job in jobs_t:
        pass_on(job, 0)
    for job in jobs_t:
        last_step(job, 0)
        first_step(job, 1)
        go(share(job, 0, c))
    for job in jobs_s:
        first_step(job, 0)
    for job in jobs_t:
        pass_on(job, 1)
        go(share(job, 3, c))
        go(share(job, 1, c))
    for job in jobs_s:
        pass_on(job, 0)
    for job in jobs_t:
        last_step(job, 1)
        go(share(job, 2, c))
    for job in jobs_s:
        last_step(job, 0)
        first_step(job, 1)
        go(share(job, 0, c))

    def live_cot(f):
        cell = iota((128, 1), 0) * 0 + (2 * s + f)
        return jnp.where(cell < frames[0], cot[f].astype(f32), 0.0)

    def out_rows(o_ref, yy):
        return jnp.concatenate([o_ref[yy, d % 2, d // 2] for d in range(HEADS)], 0)

    def qkv_rows(q_ref, yy):
        return jnp.concatenate([q_ref[yy, d % 2, d // 2] for d in range(8)], 0)

    def out_back(gated, o_ref):
        total = None
        for yy in range(NY):
            term = dot(gated[:, 256 * yy:256 * yy + OW], out_rows(o_ref, yy), NT)
            total = term if total is None else total + term
        return total.astype(bf16)

    for job in jobs_t[:2]:
        share_wait(job)
    for f in range(2):
        normin[f * 128:(f + 1) * 128, :] = (live_cot(f) * mod[5:6, :]).astype(bf16)
    dout[...] = out_back(normin, o_t)
    dsend[...] = dot(pm[...], dout[...]).astype(bf16).reshape(NSEQ, 4, HEADS * HP)
    scatter(dsend, drecv, 1, 1, NSEQ)
    mrecv[s] = msend[s]
    drecv[s] = dsend[s]

    def project(q_ref):
        def body(yy, carry):
            lanes = pl.ds(pl.multiple_of(yy * QW, QW), QW)
            qkv[:, lanes] = dot(normin[...], qkv_rows(q_ref, yy)).astype(bf16)
            return carry
        lax.fori_loop(0, NY, body, 0)

    def project_back(q_ref):
        acc[...] = jnp.zeros((TOK, D), f32)

        def body(yy, carry):
            lanes = pl.ds(pl.multiple_of(yy * QW, QW), QW)
            acc[...] += dot(dqkv[:, lanes], qkv_rows(q_ref, yy), NT)
            return carry
        lax.fori_loop(0, NY, body, 0)

    def attend(masked):
        def body(b, carry):
            rows = pl.ds(pl.multiple_of(b * 128, 128), 128)
            for h in range(HEADS):
                q = qkv[rows, head_at(h):head_at(h) + HDIM]
                k = qkv[rows, head_at(8 + h):head_at(8 + h) + HDIM]
                scores = dot(q, k, NT) * HDIM ** -0.5
                if masked:
                    scores = jnp.where(iota((128, 128), 1) < frames[0], scores, -1e30)
                e = jnp.exp(scores - jnp.max(scores, -1, keepdims=True))
                probs[b * HEADS + h] = e / jnp.sum(e, -1, keepdims=True)
            return carry
        lax.fori_loop(0, 2, body, 0)

    def attend_back():
        def body(b, carry):
            rows = pl.ds(pl.multiple_of(b * 128, 128), 128)
            for h in range(HEADS):
                q = qkv[rows, head_at(h):head_at(h) + HDIM]
                k = qkv[rows, head_at(8 + h):head_at(8 + h) + HDIM]
                v = qkv[rows, head_at(16 + h):head_at(16 + h) + HDIM]
                up = dout[rows, HP * h:HP * h + HDIM]
                p = probs[b * HEADS + h]
                dv = dot(p.astype(bf16), up, TN)
                dp_ = dot(up, v, NT)
                delta = jnp.sum(p * dp_, -1, keepdims=True)
                ds = (p * (dp_ - delta)).astype(bf16)
                dq = dot(ds, k) * HDIM ** -0.5
                dk = dot(ds, q, TN) * HDIM ** -0.5
                dqkv[rows, head_at(h):head_at(h) + HDIM] = dq.astype(bf16)
                dqkv[rows, head_at(8 + h):head_at(8 + h) + HDIM] = dk.astype(bf16)
                dqkv[rows, head_at(16 + h):head_at(16 + h) + HDIM] = dv.astype(bf16)
            return carry
        lax.fori_loop(0, 2, body, 0)

    dqkv[...] = jnp.zeros((TOK, NY * QW), bf16)

    def own_norms(i, carry):
        rows = pl.ds(pl.multiple_of(i * 64, 64), 64)
        f, r = i // 2, pl.ds(pl.multiple_of((i % 2) * 64, 64), 64)
        nm_t[rows, :], rs_t[rows, :] = norm_stats(mid[f, r, :].astype(f32))
        nm_s[rows, :], rs_s[rows, :] = norm_stats(inp[f, r, :].astype(f32))
        return carry
    lax.fori_loop(0, 4, own_norms, 0)

    wait_scatter(mrecv, arecv_sem, 0)
    acc[...] = dot(pr[...], mrecv[...].reshape(TOK, D))

    def patch_norm(i, carry):
        rows = pl.ds(pl.multiple_of(i * 64, 64), 64)
        normed, _ = norm_stats(acc[rows, :])
        normin[rows, :] = (normed * (1.0 + mod[4:5, :]) + mod[3:4, :]).astype(bf16)
        return carry
    lax.fori_loop(0, 4, patch_norm, 0)
    for job in jobs_t[2:]:
        share_wait(job)
    project(q_t)
    attend(True)
    for job in jobs_s:
        pass_on(job, 1)
        go(share(job, 3, c))
        go(share(job, 1, c))
    wait_scatter(drecv, arecv_sem, 1)
    dout[...] = dot(pr[...], drecv[...].reshape(TOK, HEADS * HP)).astype(bf16)
    attend_back()
    project_back(q_t)
    rsend[...] = dot(pr[...], acc[...].astype(bf16), TN).astype(bf16).reshape(NSEQ, 4, D)
    scatter(rsend, rrecv, 2, 1, NSEQ)
    rrecv[s] = rsend[s]

    for job in jobs_s:
        last_step(job, 1)
        go(share(job, 2, c))

    def frame_norm(i, carry):
        rows = pl.ds(pl.multiple_of(i * 64, 64), 64)
        normin[rows, :] = (nm_s[rows, :] * (1.0 + mod[1:2, :]) + mod[0:1, :]).astype(bf16)
        return carry
    lax.fori_loop(0, 4, frame_norm, 0)
    for job in jobs_s:
        share_wait(job)
    project(q_s)
    attend(False)

    wait_scatter(rrecv, arecv_sem, 2)
    acc[...] = dot(pm[...], rrecv[...].reshape(TOK, D), TN)

    def mid_grad(i, carry):
        rows = pl.ds(pl.multiple_of(i * 64, 64), 64)
        f, r = i // 2, pl.ds(pl.multiple_of((i % 2) * 64, 64), 64)
        cell = iota((64, 1), 0) * 0 + (2 * s + f)
        masked = jnp.where(cell < frames[0], cot[f, r, :].astype(f32), 0.0)
        grad = masked + norm_back(acc[rows, :], nm_t[rows, :], rs_t[rows, :], 1.0 + mod[4:5, :])
        dmid[rows, :] = grad
        normin[rows, :] = (grad * mod[2:3, :]).astype(bf16)
        return carry
    lax.fori_loop(0, 4, mid_grad, 0)
    dout[...] = out_back(normin, o_s)
    attend_back()
    project_back(q_s)

    def last_grad(i, carry):
        rows = pl.ds(pl.multiple_of(i * 64, 64), 64)
        f, r = i // 2, pl.ds(pl.multiple_of((i % 2) * 64, 64), 64)
        dnorm = acc[rows, :].astype(bf16).astype(f32)
        grad = norm_back(dnorm, nm_s[rows, :], rs_s[rows, :], 1.0 + mod[1:2, :])
        result[f, r, :] = (dmid[rows, :] + grad).astype(bf16)
        return carry
    lax.fori_loop(0, 4, last_grad, 0)

    for cp in pending:
        cp.wait_send()
    wait_scatter(msend, asend_sem, 0)
    wait_scatter(dsend, asend_sem, 1)
    wait_scatter(rsend, asend_sem, 2)


def per_device(inputs, mid_inputs, cotangent, modulation, frames, qkv_s, out_s, qkv_t, out_t):
    vmem = pl.BlockSpec(memory_space=pltpu.VMEM)
    dma = pltpu.SemaphoreType.DMA
    out = pl.pallas_call(
        kernel,
        out_shape=jax.ShapeDtypeStruct((2, 128, D), bf16),
        in_specs=[vmem] * 4 + [pl.BlockSpec(memory_space=pltpu.SMEM)] + [vmem] * 4,
        out_specs=vmem,
        scratch_shapes=[
            pltpu.VMEM((NZ, 128, 128), bf16),
            pltpu.VMEM((NZ, 224, QW), bf16),
            pltpu.VMEM((NZ, 224, OW), bf16),
            pltpu.VMEM((NY, 2, NX, 144, QW), bf16),
            pltpu.VMEM((NY, 2, NX, HP, OW), bf16),
            pltpu.VMEM((NY, 2, NX, 144, QW), bf16),
            pltpu.VMEM((NY, 2, NX, HP, OW), bf16),
            pltpu.VMEM((NSEQ, 4, D), bf16),
            pltpu.VMEM((NSEQ, 4, D), bf16),
            pltpu.VMEM((NSEQ, 4, HEADS * HP), bf16),
            pltpu.VMEM((NSEQ, 4, HEADS * HP), bf16),
            pltpu.VMEM((NSEQ, 4, D), bf16),
            pltpu.VMEM((NSEQ, 4, D), bf16),
            pltpu.VMEM((TOK, TOK), bf16),
            pltpu.VMEM((TOK, TOK), bf16),
            pltpu.VMEM((TOK, D), bf16),
            pltpu.VMEM((TOK, NY * QW), bf16),
            pltpu.VMEM((TOK, NY * QW), bf16),
            pltpu.VMEM((TOK, HEADS * HP), bf16),
            pltpu.VMEM((2 * HEADS, 128, 128), f32),
            pltpu.VMEM((TOK, D), f32),
            pltpu.VMEM((TOK, D), f32),
            pltpu.VMEM((TOK, 1), f32),
            pltpu.VMEM((TOK, D), f32),
            pltpu.VMEM((TOK, 1), f32),
            pltpu.VMEM((TOK, D), f32),
            dma((2, 8)), dma((2, 8)), dma((8, 12)), dma((8, 12)), dma((3,)), dma((3,)),
        ],
        compiler_params=pltpu.CompilerParams(
            collective_id=0, has_side_effects=True, vmem_limit_bytes=56 * 1024 * 1024
        ),
        name="blocks_grad",
    )(
        inputs[0], mid_inputs[0], cotangent[0], modulation[0], frames,
        qkv_s.T, out_s, qkv_t.T, out_t,
    )
    return out[None]


def solution(mesh):
    big = P("dp", "seq", None, None)
    weight = P("dp", "seq")
    return jax.shard_map(
        per_device,
        mesh=mesh,
        in_specs=(big, big, big, P("dp", None, None), P("dp")) + (weight,) * 4,
        out_specs=big,
        check_vma=False,
    )
```

time: 649 us -> 160 us (0.25)
  the two profiles are of different devices: /device:TPU:1 before, /device:TPU:8 now
where the time goes in v1:
time: 160 us
  Pallas kernels  155 us (97%)
  local copies, waits for them, and re-layouts  3.96 us (2%)
    pallas_call x1, Pallas kernels, per_device(): pl.pallas_call(kernel, out_shape=jax.ShapeDtypeStruct((2, 128, D), bf16),...  155 us
    unnamed x10, local copies, waits for them, and re-layouts  3.96 us

profile of v1, /device:TPU:8, one launch (start us, length us, event | category | flops | bytes accessed | tf_op | source)
XLA Modules:
  0.0 159.9 jit_solution(6684521538148979258)
XLA Ops:
  0.0 0.0 copy-start.1
  0.7 0.0 copy-start.2
  0.7 0.0 copy-start
  0.7 0.0 copy-done.1
  0.7 0.7 copy.10.out_s
  1.4 0.0 copy-done.2
  1.4 0.7 copy.11.out_t
  2.1 0.0 copy-done
  2.1 0.6 copy.14
  2.7 155.3 %blocks_grad.1 = bf16[2,128,1152]{2,1,0:T(8,128)(2,1)} custom-call(bf16[2,128,1152]{2,1,0:T(8,128)(2,1)} %bitcast.10, bf16[2,128,1152]{2,1,0:T(8,128)(2,1)} %bitcast.11, bf16[2,128,1152]{2,1,0:T(8,128)(2,1)} %bitcast.12, f32[6,1152]{1,0:T(8,128)} %bitcast.13, s32[1]{0:T(128)S(6)} %copy.16.frames, bf16[27,144]{1,0:T(8,128)(2,1)} %bitcast.14, ...), custom_call_target="tpu_custom_call" | custom-call | tf_op jit(solution)/shard_map/blocks_grad/pallas_call | solution.py:429
  158.0 1.9 %copy.17 = bf16[1,2,128,1152]{3,2,1,0:T(8,128)(2,1)} copy(bf16[1,2,128,1152]{3,2,1,0:T(8,128)(2,1)} %bitcast.9) | data formatting | bytes 1179648
Async XLA Ops:
  0.0 0.7 copy-start.1
  0.7 0.7 copy-start.2
  0.7 1.4 copy-start

commit v2 on v1

--- a/solution.py
+++ b/solution.py
@@ -55,7 +55,7 @@
     inp, mid, cot, mod, frames, qkv_s, out_s, qkv_t, out_t, result,
     zbuf, eq, eo, q_t, o_t, q_s, o_s,
     msend, mrecv, dsend, drecv, rsend, rrecv,
-    pm, pr, normin, qkv, dqkv, dout, probs, acc, nm_t, rs_t, nm_s, rs_s, dmid,
+    pm, pr, back, normin, qkv, dqkv, dout, probs, acc, nm_t, rs_t, nm_s, rs_s, dmid,
     zsend_sem, zrecv_sem, jsend_sem, jrecv_sem, asend_sem, arecv_sem,
 ):
     dp = lax.axis_index("dp")
@@ -72,9 +72,10 @@
         return {"dp": xx * 2 + c}
 
     def peer(j):
-        t = j // 4
-        dz = jnp.where(t % 2 == 1, (t + 1) // 2, NZ - t // 2)
-        return ((y + j % 4) % NY) * NZ + (z + dz) % NZ
+        near = 7 - (j - 4) // 8
+        dz = jnp.where(j < 4, 8, jnp.where(j >= 60, 0, jnp.where(j % 2 == 0, near, NZ - near)))
+        dy = jnp.where((j < 4) | (j >= 60), j % 4, ((j - 4) % 8) // 2)
+        return ((y + dy) % NY) * NZ + (z + dz) % NZ
 
     barrier = pltpu.get_barrier_semaphore()
 
@@ -85,7 +86,8 @@
     for xx in ((x + 1) % NX, (x + 3) % NX):
         pl.semaphore_signal(barrier, inc=1, device_id=x_dev(xx))
     pl.semaphore_signal(barrier, inc=1, device_id={"dp": x * 2 + other})
-    lax.fori_loop(1, NSEQ, greet, 0)
+    lax.fori_loop(0, NSEQ - 4, greet, 0)
+    lax.fori_loop(NSEQ - 3, NSEQ, greet, 0)
 
     def pack(qkv_ref, out_ref):
         q, o = qkv_ref[...], out_ref[...]
@@ -97,8 +99,8 @@
         q0 = dot(q, place(27, 0), TN)[0:64]
         q1 = dot(q, place(27, 1), TN)[64:128]
         q2 = dot(q, place(27, 2), TN)[128:144]
-        o2 = dot(o, place(18, 2))[0:48]
-        o3 = dot(o, place(18, 3))[48:72]
+        o2 = dot(o, place(18, 2), TN)[0:48]
+        o3 = dot(o, place(18, 3), TN)[48:72]
         full = q0 + q1 + jnp.concatenate([q2, o2], 0)
         full = full + jnp.concatenate([o3, jnp.zeros((40, 128), f32)], 0)
         return full.astype(bf16)
@@ -112,6 +114,9 @@
         ci == ((ri & 127) >> 1) * 4 + (ri >> 7) * 2 + (ri & 1), 1.0, 0.0
     ).astype(bf16)
 
+    back[...] = jnp.where(
+        ci == (ri & 1) * 128 + ((ri & 127) >> 1) * 2 + (ri >> 7), 1.0, 0.0
+    ).astype(bf16)
     msend[...] = dot(pm[...], mid[...].reshape(TOK, D)).astype(bf16).reshape(NSEQ, 4, D)
 
     pl.semaphore_wait(barrier, NSEQ - 1 + 3)
@@ -138,6 +143,17 @@
     def wait_scatter(ref, sem, k):
         part = ref.at[pl.ds(0, NSEQ - 1)]
         pltpu.make_async_copy(part, part, sem.at[k]).wait()
+
+    def fill(zz, carry):
+        lane = iota((224, QW), 0) - 96
+        live = (lane >= 0) & (lane < 27)
+        hit = live & (iota((224, QW), 1) == lane + 27 * zz)
+        eq[zz] = jnp.where(hit, 1.0, 0.0).astype(bf16)
+        lane = iota((224, OW), 0) - 96
+        live = (lane >= 0) & (lane < 18)
+        hit = live & (iota((224, OW), 1) == lane + 18 * zz + 32 * y)
+        eo[zz] = jnp.where(hit, 1.0, 0.0).astype(bf16)
+        return carry
 
     for step in range(8):
         if step > 0:
@@ -151,19 +167,8 @@
             cp = zcopy((z + step) % NZ, 1, step)
             cp.start()
             pending.append(cp)
-            scatter(msend, mrecv, 0, 1 + 9 * step, 10 + 9 * step)
-        if step == 0:
-            def fill(zz, carry):
-                lane = iota((224, QW), 0) - 96
-                live = (lane >= 0) & (lane < 27)
-                hit = live & (iota((224, QW), 1) == lane + 27 * zz)
-                eq[zz] = jnp.where(hit, 1.0, 0.0).astype(bf16)
-                lane = iota((224, OW), 0) - 96
-                live = (lane >= 0) & (lane < 18)
-                hit = live & (iota((224, OW), 1) == lane + 18 * zz + 32 * y)
-                eo[zz] = jnp.where(hit, 1.0, 0.0).astype(bf16)
-                return carry
-            lax.fori_loop(0, NZ, fill, 0)
+        scatter(msend, mrecv, 0, 3 * step, 3 * step + 3)
+        lax.fori_loop(2 * step, 2 * step + 2, fill, 0)
     zcopy((z + NZ - 8) % NZ, 0, 7).wait_recv()
 
     def unpack(at, q_ref, o_ref):
@@ -237,32 +242,6 @@
         for rel in range(4):
             share(job, rel, other).wait_recv()
 
-    unpack(0, q_t, o_t)
-    for job in jobs_t:
-        first_step(job, 0)
-    unpack(64, q_s, o_s)
-    for job in jobs_t:
-        pass_on(job, 0)
-    for job in jobs_t:
-        last_step(job, 0)
-        first_step(job, 1)
-        go(share(job, 0, c))
-    for job in jobs_s:
-        first_step(job, 0)
-    for job in jobs_t:
-        pass_on(job, 1)
-        go(share(job, 3, c))
-        go(share(job, 1, c))
-    for job in jobs_s:
-        pass_on(job, 0)
-    for job in jobs_t:
-        last_step(job, 1)
-        go(share(job, 2, c))
-    for job in jobs_s:
-        last_step(job, 0)
-        first_step(job, 1)
-        go(share(job, 0, c))
-
     def live_cot(f):
         cell = iota((128, 1), 0) * 0 + (2 * s + f)
         return jnp.where(cell < frames[0], cot[f].astype(f32), 0.0)
@@ -280,15 +259,53 @@
             total = term if total is None else total + term
         return total.astype(bf16)
 
-    for job in jobs_t[:2]:
-        share_wait(job)
+    def open_second(job):
+        last_step(job, 0)
+        first_step(job, 1)
+        go(share(job, 0, c))
+
+    def on_second(job):
+        pass_on(job, 1)
+        go(share(job, 3, c))
+        go(share(job, 1, c))
+
+    def end_second(job):
+        last_step(job, 1)
+        go(share(job, 2, c))
+
+    def each(f, jobs, *args):
+        for job in jobs:
+            f(job, *args)
+
+    jobs_o, jobs_q = jobs_t[:2], jobs_t[2:]
+    unpack(0, q_t, o_t)
+    each(first_step, jobs_t, 0)
+    scatter(msend, mrecv, 0, 24, 37)
+    unpack(64, q_s, o_s)
+    each(pass_on, jobs_o, 0)
+    each(open_second, jobs_o)
+    each(pass_on, jobs_q, 0)
+    scatter(msend, mrecv, 0, 37, 50)
+    each(on_second, jobs_o)
+    each(open_second, jobs_q)
+    scatter(msend, mrecv, 0, 50, 60)
+    scatter(msend, mrecv, 0, 61, 64)
+    each(end_second, jobs_o)
+    each(first_step, jobs_s, 0)
+
+    each(share_wait, jobs_o)
     for f in range(2):
-        normin[f * 128:(f + 1) * 128, :] = (live_cot(f) * mod[5:6, :]).astype(bf16)
+        normin[f * 128:(f + 1) * 128, :] = (live_cot(f) * mod[5]).astype(bf16)
     dout[...] = out_back(normin, o_t)
     dsend[...] = dot(pm[...], dout[...]).astype(bf16).reshape(NSEQ, 4, HEADS * HP)
-    scatter(dsend, drecv, 1, 1, NSEQ)
+    scatter(dsend, drecv, 1, 0, 60)
+    scatter(dsend, drecv, 1, 61, 64)
     mrecv[s] = msend[s]
     drecv[s] = dsend[s]
+    each(on_second, jobs_q)
+    each(pass_on, jobs_s, 0)
+    each(end_second, jobs_q)
+    each(open_second, jobs_s)
 
     def project(q_ref):
         def body(yy, carry):
@@ -297,12 +314,12 @@
             return carry
         lax.fori_loop(0, NY, body, 0)
 
-    def project_back(q_ref):
-        acc[...] = jnp.zeros((TOK, D), f32)
+    def project_back(q_ref, lo, n):
+        acc[lo:lo + n, :] = jnp.zeros((n, D), f32)
 
         def body(yy, carry):
             lanes = pl.ds(pl.multiple_of(yy * QW, QW), QW)
-            acc[...] += dot(dqkv[:, lanes], qkv_rows(q_ref, yy), NT)
+            acc[lo:lo + n, :] += dot(dqkv[lo:lo + n, lanes], qkv_rows(q_ref, yy), NT)
             return carry
         lax.fori_loop(0, NY, body, 0)
 
@@ -320,7 +337,7 @@
             return carry
         lax.fori_loop(0, 2, body, 0)
 
-    def attend_back():
+    def attend_back(lo, hi):
         def body(b, carry):
             rows = pl.ds(pl.multiple_of(b * 128, 128), 128)
             for h in range(HEADS):
@@ -339,7 +356,7 @@
                 dqkv[rows, head_at(8 + h):head_at(8 + h) + HDIM] = dk.astype(bf16)
                 dqkv[rows, head_at(16 + h):head_at(16 + h) + HDIM] = dv.astype(bf16)
             return carry
-        lax.fori_loop(0, 2, body, 0)
+        lax.fori_loop(lo, hi, body, 0)
 
     dqkv[...] = jnp.zeros((TOK, NY * QW), bf16)
 
@@ -357,61 +374,57 @@
     def patch_norm(i, carry):
         rows = pl.ds(pl.multiple_of(i * 64, 64), 64)
         normed, _ = norm_stats(acc[rows, :])
-        normin[rows, :] = (normed * (1.0 + mod[4:5, :]) + mod[3:4, :]).astype(bf16)
+        normin[rows, :] = (normed * (1.0 + mod[4]) + mod[3]).astype(bf16)
         return carry
     lax.fori_loop(0, 4, patch_norm, 0)
-    for job in jobs_t[2:]:
-        share_wait(job)
+    each(share_wait, jobs_q)
     project(q_t)
     attend(True)
-    for job in jobs_s:
-        pass_on(job, 1)
-        go(share(job, 3, c))
-        go(share(job, 1, c))
+    each(on_second, jobs_s)
     wait_scatter(drecv, arecv_sem, 1)
     dout[...] = dot(pr[...], drecv[...].reshape(TOK, HEADS * HP)).astype(bf16)
-    attend_back()
-    project_back(q_t)
-    rsend[...] = dot(pr[...], acc[...].astype(bf16), TN).astype(bf16).reshape(NSEQ, 4, D)
-    scatter(rsend, rrecv, 2, 1, NSEQ)
-    rrecv[s] = rsend[s]
-
-    for job in jobs_s:
-        last_step(job, 1)
-        go(share(job, 2, c))
+    for b in range(2):
+        attend_back(b, b + 1)
+        project_back(q_t, 128 * b, 128)
+        rsend[b] = acc[128 * b:128 * b + 128, :].astype(bf16).reshape(NSEQ, 2, D)
+        scatter(rsend.at[b], rrecv.at[b], 2 + b, 0, 60)
+        scatter(rsend.at[b], rrecv.at[b], 2 + b, 61, 64)
+        rrecv[b, s] = rsend[b, s]
+
+    each(end_second, jobs_s)
 
     def frame_norm(i, carry):
         rows = pl.ds(pl.multiple_of(i * 64, 64), 64)
-        normin[rows, :] = (nm_s[rows, :] * (1.0 + mod[1:2, :]) + mod[0:1, :]).astype(bf16)
+        normin[rows, :] = (nm_s[rows, :] * (1.0 + mod[1]) + mod[0]).astype(bf16)
         return carry
     lax.fori_loop(0, 4, frame_norm, 0)
-    for job in jobs_s:
-        share_wait(job)
+    each(share_wait, jobs_s)
     project(q_s)
     attend(False)
 
-    wait_scatter(rrecv, arecv_sem, 2)
-    acc[...] = dot(pm[...], rrecv[...].reshape(TOK, D), TN)
+    for b in range(2):
+        wait_scatter(rrecv.at[b], arecv_sem, 2 + b)
+    acc[...] = dot(back[...], rrecv[...].reshape(TOK, D))
 
     def mid_grad(i, carry):
         rows = pl.ds(pl.multiple_of(i * 64, 64), 64)
         f, r = i // 2, pl.ds(pl.multiple_of((i % 2) * 64, 64), 64)
         cell = iota((64, 1), 0) * 0 + (2 * s + f)
         masked = jnp.where(cell < frames[0], cot[f, r, :].astype(f32), 0.0)
-        grad = masked + norm_back(acc[rows, :], nm_t[rows, :], rs_t[rows, :], 1.0 + mod[4:5, :])
+        grad = masked + norm_back(acc[rows, :], nm_t[rows, :], rs_t[rows, :], 1.0 + mod[4])
         dmid[rows, :] = grad
-        normin[rows, :] = (grad * mod[2:3, :]).astype(bf16)
+        normin[rows, :] = (grad * mod[2]).astype(bf16)
         return carry
     lax.fori_loop(0, 4, mid_grad, 0)
     dout[...] = out_back(normin, o_s)
-    attend_back()
-    project_back(q_s)
+    attend_back(0, 2)
+    project_back(q_s, 0, TOK)
 
     def last_grad(i, carry):
         rows = pl.ds(pl.multiple_of(i * 64, 64), 64)
         f, r = i // 2, pl.ds(pl.multiple_of((i % 2) * 64, 64), 64)
         dnorm = acc[rows, :].astype(bf16).astype(f32)
-        grad = norm_back(dnorm, nm_s[rows, :], rs_s[rows, :], 1.0 + mod[1:2, :])
+        grad = norm_back(dnorm, nm_s[rows, :], rs_s[rows, :], 1.0 + mod[1])
         result[f, r, :] = (dmid[rows, :] + grad).astype(bf16)
         return carry
     lax.fori_loop(0, 4, last_grad, 0)
@@ -420,7 +433,8 @@
         cp.wait_send()
     wait_scatter(msend, asend_sem, 0)
     wait_scatter(dsend, asend_sem, 1)
-    wait_scatter(rsend, asend_sem, 2)
+    for b in range(2):
+        wait_scatter(rsend.at[b], asend_sem, 2 + b)
 
 
 def per_device(inputs, mid_inputs, cotangent, modulation, frames, qkv_s, out_s, qkv_t, out_t):
@@ -443,8 +457,9 @@
             pltpu.VMEM((NSEQ, 4, D), bf16),
             pltpu.VMEM((NSEQ, 4, HEADS * HP), bf16),
             pltpu.VMEM((NSEQ, 4, HEADS * HP), bf16),
-            pltpu.VMEM((NSEQ, 4, D), bf16),
-            pltpu.VMEM((NSEQ, 4, D), bf16),
+            pltpu.VMEM((2, NSEQ, 2, D), bf16),
+            pltpu.VMEM((2, NSEQ, 2, D), bf16),
+            pltpu.VMEM((TOK, TOK), bf16),
             pltpu.VMEM((TOK, TOK), bf16),
             pltpu.VMEM((TOK, TOK), bf16),
             pltpu.VMEM((TOK, D), bf16),
@@ -458,15 +473,15 @@
             pltpu.VMEM((TOK, D), f32),
             pltpu.VMEM((TOK, 1), f32),
             pltpu.VMEM((TOK, D), f32),
-            dma((2, 8)), dma((2, 8)), dma((8, 12)), dma((8, 12)), dma((3,)), dma((3,)),
+            dma((2, 8)), dma((2, 8)), dma((8, 12)), dma((8, 12)), dma((4,)), dma((4,)),
         ],
         compiler_params=pltpu.CompilerParams(
             collective_id=0, has_side_effects=True, vmem_limit_bytes=56 * 1024 * 1024
         ),
         name="blocks_grad",
     )(
-        inputs[0], mid_inputs[0], cotangent[0], modulation[0], frames,
-        qkv_s.T, out_s, qkv_t.T, out_t,
+        inputs[0], mid_inputs[0], cotangent[0], modulation.reshape(6, 1, D), frames,
+        qkv_s.T, out_s.T, qkv_t.T, out_t.T,
     )
     return out[None]
 

time: 160 us -> 141 us (0.88)
  the two profiles are of different devices: /device:TPU:8 before, /device:TPU:1 now
where the time goes in v2:
time: 141 us
  Pallas kernels  138 us (98%)
  local copies, waits for them, and re-layouts  1.92 us (1%)
    pallas_call x1, Pallas kernels, per_device(): pl.pallas_call(kernel, out_shape=jax.ShapeDtypeStruct((2, 128, D), bf16),...  138 us

profile of v2, /device:TPU:1, one launch (start us, length us, event | category | flops | bytes accessed | tf_op | source)
XLA Modules:
  0.0 140.9 jit_solution(1390015985872514111)
XLA Ops:
  0.7 138.4 %blocks_grad.1 = bf16[2,128,1152]{2,1,0:T(8,128)(2,1)} custom-call(bf16[2,128,1152]{2,1,0:T(8,128)(2,1)} %bitcast.10, bf16[2,128,1152]{2,1,0:T(8,128)(2,1)} %bitcast.11, bf16[2,128,1152]{2,1,0:T(8,128)(2,1)} %bitcast.12, f32[6,1,1152]{2,1,0:T(1,128)} %bitcast.13, s32[1]{0:T(128)S(6)} %copy.11.frames, bf16[27,144]{1,0:T(8,128)(2,1)} %bitcast.14, ...), custom_call_target="tpu_custom_call" | custom-call | tf_op jit(solution)/shard_map/blocks_grad/pallas_call | solution.py:443
  139.0 1.9 %copy.12 = bf16[1,2,128,1152]{3,2,1,0:T(8,128)(2,1)} copy(bf16[1,2,128,1152]{3,2,1,0:T(8,128)(2,1)} %bitcast.9) | data formatting | bytes 1179648

commit v3 on v2

--- a/solution.py
+++ b/solution.py
@@ -71,23 +71,32 @@
     def x_dev(xx):
         return {"dp": xx * 2 + c}
 
-    def peer(j):
-        near = 7 - (j - 4) // 8
-        dz = jnp.where(j < 4, 8, jnp.where(j >= 60, 0, jnp.where(j % 2 == 0, near, NZ - near)))
-        dy = jnp.where((j < 4) | (j >= 60), j % 4, ((j - 4) % 8) // 2)
-        return ((y + dy) % NY) * NZ + (z + dz) % NZ
+    far = [(8, dy) for dy in range(NY)]
+    near = [(dz, dy) for dy in range(NY) for dz in (0, 1)]
+    beside = [(0, dy) for dy in range(1, NY)]
+
+    def peer(dz, dy):
+        return lax.rem(y + dy, NY) * NZ + lax.rem(z + dz, NZ)
+
+    def each_peer(f):
+        for dz, dy in far:
+            f(peer(dz, dy))
+
+        def body(i, carry):
+            at = (lax.rem(z + 7 - i, NZ), lax.rem(z + NZ - 7 + i, NZ))
+            for way, dy in near:
+                f(lax.rem(y + dy, NY) * NZ + at[way])
+            return carry
+        lax.fori_loop(0, 7, body, 0)
+        for dz, dy in beside:
+            f(peer(dz, dy))
 
     barrier = pltpu.get_barrier_semaphore()
-
-    def greet(j, carry):
-        pl.semaphore_signal(barrier, inc=1, device_id={"seq": peer(j)})
-        return carry
 
     for xx in ((x + 1) % NX, (x + 3) % NX):
         pl.semaphore_signal(barrier, inc=1, device_id=x_dev(xx))
     pl.semaphore_signal(barrier, inc=1, device_id={"dp": x * 2 + other})
-    lax.fori_loop(0, NSEQ - 4, greet, 0)
-    lax.fori_loop(NSEQ - 3, NSEQ, greet, 0)
+    each_peer(lambda to: pl.semaphore_signal(barrier, inc=1, device_id={"seq": to}))
 
     def pack(qkv_ref, out_ref):
         q, o = qkv_ref[...], out_ref[...]
@@ -129,16 +138,21 @@
             device_id=seq_dev(y, to),
         )
 
-    def scatter(src, dst, k, lo, hi):
-        def one(j, carry):
-            to = peer(j)
-            pltpu.make_async_remote_copy(
-                src_ref=src.at[to], dst_ref=dst.at[s],
-                send_sem=asend_sem.at[k], recv_sem=arecv_sem.at[k],
-                device_id={"seq": to},
-            ).start()
-            return carry
-        lax.fori_loop(lo, hi, one, 0)
+    def send_to(src, dst, k, to):
+        pltpu.make_async_remote_copy(
+            src_ref=src.at[to], dst_ref=dst.at[s],
+            send_sem=asend_sem.at[k], recv_sem=arecv_sem.at[k],
+            device_id={"seq": to},
+        ).start()
+
+    def scatter(src, dst, k):
+        each_peer(lambda to: send_to(src, dst, k, to))
+
+    order = far + [(d, dy) for m in range(7, 0, -1) for dy in range(NY) for d in (m, NZ - m)] + beside
+
+    def send_mid(lo, hi):
+        for dz, dy in order[lo:hi]:
+            send_to(msend, mrecv, 0, peer(dz, dy))
 
     def wait_scatter(ref, sem, k):
         part = ref.at[pl.ds(0, NSEQ - 1)]
@@ -167,7 +181,7 @@
             cp = zcopy((z + step) % NZ, 1, step)
             cp.start()
             pending.append(cp)
-        scatter(msend, mrecv, 0, 3 * step, 3 * step + 3)
+        send_mid(3 * step, 3 * step + 3)
         lax.fori_loop(2 * step, 2 * step + 2, fill, 0)
     zcopy((z + NZ - 8) % NZ, 0, 7).wait_recv()
 
@@ -280,16 +294,15 @@
     jobs_o, jobs_q = jobs_t[:2], jobs_t[2:]
     unpack(0, q_t, o_t)
     each(first_step, jobs_t, 0)
-    scatter(msend, mrecv, 0, 24, 37)
+    send_mid(24, 37)
     unpack(64, q_s, o_s)
     each(pass_on, jobs_o, 0)
     each(open_second, jobs_o)
     each(pass_on, jobs_q, 0)
-    scatter(msend, mrecv, 0, 37, 50)
+    send_mid(37, 50)
     each(on_second, jobs_o)
     each(open_second, jobs_q)
-    scatter(msend, mrecv, 0, 50, 60)
-    scatter(msend, mrecv, 0, 61, 64)
+    send_mid(50, 63)
     each(end_second, jobs_o)
     each(first_step, jobs_s, 0)
 
@@ -297,11 +310,12 @@
     for f in range(2):
         normin[f * 128:(f + 1) * 128, :] = (live_cot(f) * mod[5]).astype(bf16)
     dout[...] = out_back(normin, o_t)
-    dsend[...] = dot(pm[...], dout[...]).astype(bf16).reshape(NSEQ, 4, HEADS * HP)
-    scatter(dsend, drecv, 1, 0, 60)
-    scatter(dsend, drecv, 1, 61, 64)
+    for b in range(2):
+        part = dot(back[128 * b:128 * b + 128, :], dout[...])
+        dsend[b] = part.astype(bf16).reshape(NSEQ, 2, HEADS * HP)
+        scatter(dsend.at[b], drecv.at[b], 1 + b)
+        drecv[b, s] = dsend[b, s]
     mrecv[s] = msend[s]
-    drecv[s] = dsend[s]
     each(on_second, jobs_q)
     each(pass_on, jobs_s, 0)
     each(end_second, jobs_q)
@@ -380,16 +394,16 @@
     each(share_wait, jobs_q)
     project(q_t)
     attend(True)
-    each(on_second, jobs_s)
-    wait_scatter(drecv, arecv_sem, 1)
-    dout[...] = dot(pr[...], drecv[...].reshape(TOK, HEADS * HP)).astype(bf16)
     for b in range(2):
+        wait_scatter(drecv.at[b], arecv_sem, 1 + b)
+        dout[128 * b:128 * b + 128, :] = drecv[b].reshape(128, HEADS * HP)
         attend_back(b, b + 1)
         project_back(q_t, 128 * b, 128)
         rsend[b] = acc[128 * b:128 * b + 128, :].astype(bf16).reshape(NSEQ, 2, D)
-        scatter(rsend.at[b], rrecv.at[b], 2 + b, 0, 60)
-        scatter(rsend.at[b], rrecv.at[b], 2 + b, 61, 64)
+        scatter(rsend.at[b], rrecv.at[b], 3 + b)
         rrecv[b, s] = rsend[b, s]
+        if b == 0:
+            each(on_second, jobs_s)
 
     each(end_second, jobs_s)
 
@@ -403,7 +417,7 @@
     attend(False)
 
     for b in range(2):
-        wait_scatter(rrecv.at[b], arecv_sem, 2 + b)
+        wait_scatter(rrecv.at[b], arecv_sem, 3 + b)
     acc[...] = dot(back[...], rrecv[...].reshape(TOK, D))
 
     def mid_grad(i, carry):
@@ -432,9 +446,9 @@
     for cp in pending:
         cp.wait_send()
     wait_scatter(msend, asend_sem, 0)
-    wait_scatter(dsend, asend_sem, 1)
     for b in range(2):
-        wait_scatter(rsend.at[b], asend_sem, 2 + b)
+        wait_scatter(dsend.at[b], asend_sem, 1 + b)
+        wait_scatter(rsend.at[b], asend_sem, 3 + b)
 
 
 def per_device(inputs, mid_inputs, cotangent, modulation, frames, qkv_s, out_s, qkv_t, out_t):
@@ -455,8 +469,8 @@
             pltpu.VMEM((NY, 2, NX, HP, OW), bf16),
             pltpu.VMEM((NSEQ, 4, D), bf16),
             pltpu.VMEM((NSEQ, 4, D), bf16),
-            pltpu.VMEM((NSEQ, 4, HEADS * HP), bf16),
-            pltpu.VMEM((NSEQ, 4, HEADS * HP), bf16),
+            pltpu.VMEM((2, NSEQ, 2, HEADS * HP), bf16),
+            pltpu.VMEM((2, NSEQ, 2, HEADS * HP), bf16),
             pltpu.VMEM((2, NSEQ, 2, D), bf16),
             pltpu.VMEM((2, NSEQ, 2, D), bf16),
             pltpu.VMEM((TOK, TOK), bf16),
@@ -473,10 +487,10 @@
             pltpu.VMEM((TOK, D), f32),
             pltpu.VMEM((TOK, 1), f32),
             pltpu.VMEM((TOK, D), f32),
-            dma((2, 8)), dma((2, 8)), dma((8, 12)), dma((8, 12)), dma((4,)), dma((4,)),
+            dma((2, 8)), dma((2, 8)), dma((8, 12)), dma((8, 12)), dma((5,)), dma((5,)),
         ],
         compiler_params=pltpu.CompilerParams(
-            collective_id=0, has_side_effects=True, vmem_limit_bytes=56 * 1024 * 1024
+            collective_id=0, has_side_effects=True, vmem_limit_bytes=42 * 1024 * 1024
         ),
         name="blocks_grad",
     )(

time: 141 us -> 137 us (0.972)
  Pallas kernels: 138 us -> 129 us
  local copies, waits for them, and re-layouts: 1.92 us -> 6.93 us
    pallas_call x1, Pallas kernels: 138 us -> 129 us  [per_device(): pl.pallas_call(kernel, out_shape=jax.ShapeDtypeStruct((2, 128, D), bf16),...]
    unnamed x1 -> x17, local copies, waits for them, and re-layouts: 1.92 us -> 6.93 us
where the time goes in v3:
time: 137 us
  Pallas kernels  129 us (94%)
  local copies, waits for them, and re-layouts  6.93 us (5%)
    pallas_call x1, Pallas kernels, per_device(): pl.pallas_call(kernel, out_shape=jax.ShapeDtypeStruct((2, 128, D), bf16),...  129 us
    unnamed x17, local copies, waits for them, and re-layouts  6.93 us

profile of v3, /device:TPU:1, one launch (start us, length us, event | category | flops | bytes accessed | tf_op | source)
XLA Modules:
  0.0 136.6 jit_solution(14172822114460491736)
XLA Ops:
  0.0 0.0 copy-start.4
  0.7 0.1 copy-done.4
  0.7 0.0 copy-start
  0.7 1.1 copy-done
  1.8 0.0 copy-start.1
  1.8 1.1 copy-done.1
  2.9 0.0 copy-start.2
  2.9 1.1 copy-done.2
  3.9 0.0 copy-start.3
  3.9 0.7 copy-done.3
  4.7 0.0 copy-start.5
  4.7 0.7 copy-done.5
  5.4 0.0 copy-start.6
  5.4 0.7 copy-done.6
  6.1 0.0 copy-start.7
  6.1 0.7 copy-done.7
  6.8 129.0 %blocks_grad.1 = bf16[2,128,1152]{2,1,0:T(8,128)(2,1)S(1)} custom-call(bf16[2,128,1152]{2,1,0:T(8,128)(2,1)S(1)} %bitcast.10, bf16[2,128,1152]{2,1,0:T(8,128)(2,1)S(1)} %bitcast.11, bf16[2,128,1152]{2,1,0:T(8,128)(2,1)S(1)} %bitcast.12, f32[6,1,1152]{2,1,0:T(1,128)S(1)} %bitcast.13, s32[1]{0:T(128)S(6)} %copy.11.frames, bf16[27,144]{1,0:T(8,128)(2,1)S(1)} %bitcast.14, ...), custom_call_target="tpu_custom_call" | custom-call | tf_op jit(solution)/shard_map/blocks_grad/pallas_call | solution.py:457
  135.8 0.8 copy.12
Async XLA Ops:
  0.0 0.7 copy-start.4
  0.7 1.1 copy-start
  1.8 1.1 copy-start.1
  2.9 1.1 copy-start.2
  3.9 0.7 copy-start.3
  4.7 0.7 copy-start.5
  5.4 0.7 copy-start.6
  6.1 0.7 copy-start.7

commit v4 on v3

--- a/solution.py
+++ b/solution.py
@@ -52,7 +52,8 @@
 
 
 def kernel(
-    inp, mid, cot, mod, frames, qkv_s, out_s, qkv_t, out_t, result,
+    inp_hbm, mid_hbm, cot_hbm, mod_hbm, frames, qkv_s_hbm, out_s_hbm, qkv_t_hbm, out_t_hbm, result,
+    inp, mid, cot, mod, qkv_s, out_s, qkv_t, out_t, load_sem,
     zbuf, eq, eo, q_t, o_t, q_s, o_s,
     msend, mrecv, dsend, drecv, rsend, rrecv,
     pm, pr, back, normin, qkv, dqkv, dout, probs, acc, nm_t, rs_t, nm_s, rs_s, dmid,
@@ -65,6 +66,16 @@
     other = 1 - c
     pending = []
 
+    loads = [
+        pltpu.make_async_copy(src, dst, load_sem.at[i])
+        for i, (src, dst) in enumerate((
+            (qkv_t_hbm, qkv_t), (out_t_hbm, out_t), (qkv_s_hbm, qkv_s), (out_s_hbm, out_s),
+            (mid_hbm, mid), (cot_hbm, cot), (mod_hbm, mod), (inp_hbm, inp),
+        ))
+    ]
+    for cp in loads:
+        cp.start()
+
     def seq_dev(yy, zz):
         return {"seq": yy * NZ + zz}
 
@@ -114,8 +125,10 @@
         full = full + jnp.concatenate([o3, jnp.zeros((40, 128), f32)], 0)
         return full.astype(bf16)
 
-    zbuf[z, 0:64] = pack(qkv_t, out_t)
-    zbuf[z, 64:128] = pack(qkv_s, out_s)
+    for cp in loads[:4]:
+        cp.wait()
+    zbuf[z, 0] = pack(qkv_t, out_t)
+    zbuf[z, 1] = pack(qkv_s, out_s)
 
     ri, ci = iota((TOK, TOK), 0), iota((TOK, TOK), 1)
     pm[...] = jnp.where(ci == (ri & 1) * 128 + (ri >> 2) * 2 + ((ri >> 1) & 1), 1.0, 0.0).astype(bf16)
@@ -126,17 +139,28 @@
     back[...] = jnp.where(
         ci == (ri & 1) * 128 + ((ri & 127) >> 1) * 2 + (ri >> 7), 1.0, 0.0
     ).astype(bf16)
+    loads[4].wait()
     msend[...] = dot(pm[...], mid[...].reshape(TOK, D)).astype(bf16).reshape(NSEQ, 4, D)
 
     pl.semaphore_wait(barrier, NSEQ - 1 + 3)
 
     def zcopy(block, way, step):
-        to = (z + 1) % NZ if way == 0 else (z + NZ - 1) % NZ
+        to = lax.rem(z + 1, NZ) if way == 0 else lax.rem(z + NZ - 1, NZ)
+        ref = zbuf.at[block]
         return pltpu.make_async_remote_copy(
-            src_ref=zbuf.at[block], dst_ref=zbuf.at[block],
+            src_ref=ref, dst_ref=ref,
             send_sem=zsend_sem.at[way, step], recv_sem=zrecv_sem.at[way, step],
             device_id=seq_dev(y, to),
         )
+
+    def ring_step(step):
+        for way, block in ((0, lax.rem(z + NZ - step, NZ)), (1, lax.rem(z + step, NZ))):
+            if step > 0 and not (way == 1 and step == 8):
+                zcopy(block, way, step - 1).wait_recv()
+            if step < 8 - way:
+                cp = zcopy(block, way, step)
+                cp.start()
+                pending.append(cp)
 
     def send_to(src, dst, k, to):
         pltpu.make_async_remote_copy(
@@ -170,23 +194,13 @@
         return carry
 
     for step in range(8):
-        if step > 0:
-            zcopy((z + NZ - step) % NZ, 0, step - 1).wait_recv()
-        cp = zcopy((z + NZ - step) % NZ, 0, step)
-        cp.start()
-        pending.append(cp)
-        if step > 0:
-            zcopy((z + step) % NZ, 1, step - 1).wait_recv()
-        if step < 7:
-            cp = zcopy((z + step) % NZ, 1, step)
-            cp.start()
-            pending.append(cp)
-        send_mid(3 * step, 3 * step + 3)
+        ring_step(step)
+        send_mid(step, step + 1)
         lax.fori_loop(2 * step, 2 * step + 2, fill, 0)
-    zcopy((z + NZ - 8) % NZ, 0, 7).wait_recv()
-
-    def unpack(at, q_ref, o_ref):
-        whole = jnp.concatenate([zbuf[i, at:at + 64] for i in range(NZ)], 1)
+    ring_step(8)
+
+    def unpack(kind, q_ref, o_ref):
+        whole = jnp.concatenate([zbuf[i, kind] for i in range(NZ)], 1)
 
         def pick(table, g):
             lo = 96 - 32 * g
@@ -196,11 +210,11 @@
         q_ref[y, c, x] = jnp.concatenate([pick(eq, 0), pick(eq, 1), pick(eq, 2)[0:16]], 0)
 
     jobs_t = [
-        (0, o_t, "y", 0, 48, 32), (1, o_t, "x", 48, 32, 16),
+        (0, o_t, "y", 0, 32, 16), (1, o_t, "x", 32, 48, 32),
         (2, q_t, "y", 0, 80, 48), (3, q_t, "x", 80, 64, 32),
     ]
     jobs_s = [
-        (4, o_s, "y", 0, 48, 32), (5, o_s, "x", 48, 32, 16),
+        (4, o_s, "y", 0, 32, 16), (5, o_s, "x", 32, 48, 32),
         (6, q_s, "y", 0, 80, 48), (7, q_s, "x", 80, 64, 32),
     ]
 
@@ -294,21 +308,24 @@
     jobs_o, jobs_q = jobs_t[:2], jobs_t[2:]
     unpack(0, q_t, o_t)
     each(first_step, jobs_t, 0)
-    send_mid(24, 37)
-    unpack(64, q_s, o_s)
+    send_mid(8, 20)
+    unpack(1, q_s, o_s)
     each(pass_on, jobs_o, 0)
     each(open_second, jobs_o)
+    send_mid(20, 32)
     each(pass_on, jobs_q, 0)
-    send_mid(37, 50)
+    send_mid(32, 44)
     each(on_second, jobs_o)
     each(open_second, jobs_q)
-    send_mid(50, 63)
+    send_mid(44, 63)
+    for cp in loads[5:]:
+        cp.wait()
+    for f in range(2):
+        normin[f * 128:(f + 1) * 128, :] = (live_cot(f) * mod[5]).astype(bf16)
     each(end_second, jobs_o)
     each(first_step, jobs_s, 0)
 
     each(share_wait, jobs_o)
-    for f in range(2):
-        normin[f * 128:(f + 1) * 128, :] = (live_cot(f) * mod[5]).astype(bf16)
     dout[...] = out_back(normin, o_t)
     for b in range(2):
         part = dot(back[128 * b:128 * b + 128, :], dout[...])
@@ -337,19 +354,19 @@
             return carry
         lax.fori_loop(0, NY, body, 0)
 
-    def attend(masked):
+    def attend(masked, lo=0, hi=2):
         def body(b, carry):
             rows = pl.ds(pl.multiple_of(b * 128, 128), 128)
             for h in range(HEADS):
                 q = qkv[rows, head_at(h):head_at(h) + HDIM]
                 k = qkv[rows, head_at(8 + h):head_at(8 + h) + HDIM]
-                scores = dot(q, k, NT) * HDIM ** -0.5
+                scores = dot(k, q, NT) * HDIM ** -0.5
                 if masked:
-                    scores = jnp.where(iota((128, 128), 1) < frames[0], scores, -1e30)
-                e = jnp.exp(scores - jnp.max(scores, -1, keepdims=True))
-                probs[b * HEADS + h] = e / jnp.sum(e, -1, keepdims=True)
+                    scores = jnp.where(iota((128, 128), 0) < frames[0], scores, -1e30)
+                e = jnp.exp(scores - jnp.max(scores, 0, keepdims=True))
+                probs[b * HEADS + h] = e / jnp.sum(e, 0, keepdims=True)
             return carry
-        lax.fori_loop(0, 2, body, 0)
+        lax.fori_loop(lo, hi, body, 0)
 
     def attend_back(lo, hi):
         def body(b, carry):
@@ -360,12 +377,12 @@
                 v = qkv[rows, head_at(16 + h):head_at(16 + h) + HDIM]
                 up = dout[rows, HP * h:HP * h + HDIM]
                 p = probs[b * HEADS + h]
-                dv = dot(p.astype(bf16), up, TN)
-                dp_ = dot(up, v, NT)
-                delta = jnp.sum(p * dp_, -1, keepdims=True)
+                dv = dot(p.astype(bf16), up)
+                dp_ = dot(v, up, NT)
+                delta = jnp.sum(p * dp_, 0, keepdims=True)
                 ds = (p * (dp_ - delta)).astype(bf16)
-                dq = dot(ds, k) * HDIM ** -0.5
-                dk = dot(ds, q, TN) * HDIM ** -0.5
+                dq = dot(ds, k, TN) * HDIM ** -0.5
+                dk = dot(ds, q) * HDIM ** -0.5
                 dqkv[rows, head_at(h):head_at(h) + HDIM] = dq.astype(bf16)
                 dqkv[rows, head_at(8 + h):head_at(8 + h) + HDIM] = dk.astype(bf16)
                 dqkv[rows, head_at(16 + h):head_at(16 + h) + HDIM] = dv.astype(bf16)
@@ -393,8 +410,8 @@
     lax.fori_loop(0, 4, patch_norm, 0)
     each(share_wait, jobs_q)
     project(q_t)
-    attend(True)
     for b in range(2):
+        attend(True, b, b + 1)
         wait_scatter(drecv.at[b], arecv_sem, 1 + b)
         dout[128 * b:128 * b + 128, :] = drecv[b].reshape(128, HEADS * HP)
         attend_back(b, b + 1)
@@ -416,9 +433,10 @@
     project(q_s)
     attend(False)
 
-    for b in range(2):
-        wait_scatter(rrecv.at[b], arecv_sem, 3 + b)
-    acc[...] = dot(back[...], rrecv[...].reshape(TOK, D))
+    wait_scatter(rrecv.at[0], arecv_sem, 3)
+    acc[...] = dot(back[:, 0:128], rrecv[0].reshape(128, D))
+    wait_scatter(rrecv.at[1], arecv_sem, 4)
+    acc[...] += dot(back[:, 128:256], rrecv[1].reshape(128, D))
 
     def mid_grad(i, carry):
         rows = pl.ds(pl.multiple_of(i * 64, 64), 64)
@@ -452,15 +470,24 @@
 
 
 def per_device(inputs, mid_inputs, cotangent, modulation, frames, qkv_s, out_s, qkv_t, out_t):
-    vmem = pl.BlockSpec(memory_space=pltpu.VMEM)
+    vmem, hbm = pl.BlockSpec(memory_space=pltpu.VMEM), pl.BlockSpec(memory_space=pltpu.HBM)
     dma = pltpu.SemaphoreType.DMA
     out = pl.pallas_call(
         kernel,
         out_shape=jax.ShapeDtypeStruct((2, 128, D), bf16),
-        in_specs=[vmem] * 4 + [pl.BlockSpec(memory_space=pltpu.SMEM)] + [vmem] * 4,
+        in_specs=[hbm] * 4 + [pl.BlockSpec(memory_space=pltpu.SMEM)] + [hbm] * 4,
         out_specs=vmem,
         scratch_shapes=[
-            pltpu.VMEM((NZ, 128, 128), bf16),
+            pltpu.VMEM((2, 128, D), bf16),
+            pltpu.VMEM((2, 128, D), bf16),
+            pltpu.VMEM((2, 128, D), bf16),
+            pltpu.VMEM((6, 1, D), f32),
+            pltpu.VMEM((27, 144), bf16),
+            pltpu.VMEM((18, 72), bf16),
+            pltpu.VMEM((27, 144), bf16),
+            pltpu.VMEM((18, 72), bf16),
+            dma((8,)),
+            pltpu.VMEM((NZ, 2, 64, 128), bf16),
             pltpu.VMEM((NZ, 224, QW), bf16),
             pltpu.VMEM((NZ, 224, OW), bf16),
             pltpu.VMEM((NY, 2, NX, 144, QW), bf16),
@@ -490,7 +517,7 @@
             dma((2, 8)), dma((2, 8)), dma((8, 12)), dma((8, 12)), dma((5,)), dma((5,)),
         ],
         compiler_params=pltpu.CompilerParams(
-            collective_id=0, has_side_effects=True, vmem_limit_bytes=42 * 1024 * 1024
+            collective_id=0, has_side_effects=True, vmem_limit_bytes=56 * 1024 * 1024
         ),
         name="blocks_grad",
     )(

time: 137 us -> 130 us (0.949)
  local copies, waits for them, and re-layouts: 6.93 us -> 1.92 us
  Pallas kernels: 129 us -> 127 us
    unnamed x17 -> x1, local copies, waits for them, and re-layouts: 6.93 us -> 1.92 us
    pallas_call x1, Pallas kernels: 129 us -> 127 us  [per_device(): pl.pallas_call(kernel, out_shape=jax.ShapeDtypeStruct((2, 128, D), bf16),...]
where the time goes in v4:
time: 130 us; the launch traced here: 129 us
  Pallas kernels  127 us (98%)
  local copies, waits for them, and re-layouts  1.92 us (1%)
    pallas_call x1, Pallas kernels, per_device(): pl.pallas_call(kernel, out_shape=jax.ShapeDtypeStruct((2, 128, D), bf16),...  127 us

profile of v4, /device:TPU:1, one launch (start us, length us, event | category | flops | bytes accessed | tf_op | source)
XLA Modules:
  0.0 129.1 jit_solution(9945671957166962671)
XLA Ops:
  0.7 126.5 %blocks_grad.1 = bf16[2,128,1152]{2,1,0:T(8,128)(2,1)} custom-call(bf16[2,128,1152]{2,1,0:T(8,128)(2,1)} %bitcast.10, bf16[2,128,1152]{2,1,0:T(8,128)(2,1)} %bitcast.11, bf16[2,128,1152]{2,1,0:T(8,128)(2,1)} %bitcast.12, f32[6,1,1152]{2,1,0:T(1,128)} %bitcast.13, s32[1]{0:T(128)S(6)} %copy.11.frames, bf16[27,144]{1,0:T(8,128)(2,1)} %bitcast.14, ...), custom_call_target="tpu_custom_call" | custom-call | tf_op jit(solution)/shard_map/blocks_grad/pallas_call | solution.py:475
  127.2 1.9 %copy.12 = bf16[1,2,128,1152]{3,2,1,0:T(8,128)(2,1)} copy(bf16[1,2,128,1152]{3,2,1,0:T(8,128)(2,1)} %bitcast.9) | data formatting | bytes 1179648

commit v5 on v4

--- a/solution.py
+++ b/solution.py
@@ -139,26 +139,27 @@
     back[...] = jnp.where(
         ci == (ri & 1) * 128 + ((ri & 127) >> 1) * 2 + (ri >> 7), 1.0, 0.0
     ).astype(bf16)
+    dqkv[...] = jnp.zeros((TOK, NY * QW), bf16)
     loads[4].wait()
     msend[...] = dot(pm[...], mid[...].reshape(TOK, D)).astype(bf16).reshape(NSEQ, 4, D)
 
     pl.semaphore_wait(barrier, NSEQ - 1 + 3)
 
-    def zcopy(block, way, step):
+    def zcopy(kind, block, way, step):
         to = lax.rem(z + 1, NZ) if way == 0 else lax.rem(z + NZ - 1, NZ)
-        ref = zbuf.at[block]
+        ref = zbuf.at[block, kind]
         return pltpu.make_async_remote_copy(
             src_ref=ref, dst_ref=ref,
-            send_sem=zsend_sem.at[way, step], recv_sem=zrecv_sem.at[way, step],
+            send_sem=zsend_sem.at[kind, way, step], recv_sem=zrecv_sem.at[kind, way, step],
             device_id=seq_dev(y, to),
         )
 
-    def ring_step(step):
+    def ring_step(kind, step):
         for way, block in ((0, lax.rem(z + NZ - step, NZ)), (1, lax.rem(z + step, NZ))):
             if step > 0 and not (way == 1 and step == 8):
-                zcopy(block, way, step - 1).wait_recv()
+                zcopy(kind, block, way, step - 1).wait_recv()
             if step < 8 - way:
-                cp = zcopy(block, way, step)
+                cp = zcopy(kind, block, way, step)
                 cp.start()
                 pending.append(cp)
 
@@ -193,21 +194,44 @@
         eo[zz] = jnp.where(hit, 1.0, 0.0).astype(bf16)
         return carry
 
+    def own_norms(i, carry):
+        rows = pl.ds(pl.multiple_of(i * 64, 64), 64)
+        f, r = i // 2, pl.ds(pl.multiple_of((i % 2) * 64, 64), 64)
+        nm_t[rows, :], rs_t[rows, :] = norm_stats(mid[f, r, :].astype(f32))
+        nm_s[rows, :], rs_s[rows, :] = norm_stats(inp[f, r, :].astype(f32))
+        return carry
+
+    def live_cot(f):
+        cell = iota((128, 1), 0) * 0 + (2 * s + f)
+        return jnp.where(cell < frames[0], cot[f].astype(f32), 0.0)
+
     for step in range(8):
-        ring_step(step)
+        ring_step(0, step)
+        ring_step(1, step)
         send_mid(step, step + 1)
         lax.fori_loop(2 * step, 2 * step + 2, fill, 0)
-    ring_step(8)
-
-    def unpack(kind, q_ref, o_ref):
+        if step == 1:
+            for cp in loads[5:]:
+                cp.wait()
+        if step in (2, 3):
+            f = step - 2
+            normin[f * 128:(f + 1) * 128, :] = (live_cot(f) * mod[5]).astype(bf16)
+        if step > 3:
+            lax.fori_loop(step - 4, step - 3, own_norms, 0)
+    ring_step(0, 8)
+
+    def unpack(kind, ref):
         whole = jnp.concatenate([zbuf[i, kind] for i in range(NZ)], 1)
-
-        def pick(table, g):
+        table = eo if ref is o_t or ref is o_s else eq
+
+        def pick(g):
             lo = 96 - 32 * g
             return dot(whole, table[:, lo:lo + 128, :].reshape(NZ * 128, -1)).astype(bf16)
 
-        o_ref[y, c, x] = jnp.concatenate([pick(eo, 2)[16:64], pick(eo, 3)[0:32]], 0)
-        q_ref[y, c, x] = jnp.concatenate([pick(eq, 0), pick(eq, 1), pick(eq, 2)[0:16]], 0)
+        if table is eo:
+            ref[y, c, x] = jnp.concatenate([pick(2)[16:64], pick(3)[0:32]], 0)
+        else:
+            ref[y, c, x] = jnp.concatenate([pick(0), pick(1), pick(2)[0:16]], 0)
 
     jobs_t = [
         (0, o_t, "y", 0, 32, 16), (1, o_t, "x", 32, 48, 32),
@@ -270,10 +294,6 @@
         for rel in range(4):
             share(job, rel, other).wait_recv()
 
-    def live_cot(f):
-        cell = iota((128, 1), 0) * 0 + (2 * s + f)
-        return jnp.where(cell < frames[0], cot[f].astype(f32), 0.0)
-
     def out_rows(o_ref, yy):
         return jnp.concatenate([o_ref[yy, d % 2, d // 2] for d in range(HEADS)], 0)
 
@@ -306,10 +326,14 @@
             f(job, *args)
 
     jobs_o, jobs_q = jobs_t[:2], jobs_t[2:]
-    unpack(0, q_t, o_t)
-    each(first_step, jobs_t, 0)
+    unpack(0, o_t)
+    each(first_step, jobs_o, 0)
+    unpack(0, q_t)
+    each(first_step, jobs_q, 0)
     send_mid(8, 20)
-    unpack(1, q_s, o_s)
+    ring_step(1, 8)
+    unpack(1, o_s)
+    unpack(1, q_s)
     each(pass_on, jobs_o, 0)
     each(open_second, jobs_o)
     send_mid(20, 32)
@@ -318,10 +342,6 @@
     each(on_second, jobs_o)
     each(open_second, jobs_q)
     send_mid(44, 63)
-    for cp in loads[5:]:
-        cp.wait()
-    for f in range(2):
-        normin[f * 128:(f + 1) * 128, :] = (live_cot(f) * mod[5]).astype(bf16)
     each(end_second, jobs_o)
     each(first_step, jobs_s, 0)
 
@@ -334,14 +354,12 @@
         drecv[b, s] = dsend[b, s]
     mrecv[s] = msend[s]
     each(on_second, jobs_q)
-    each(pass_on, jobs_s, 0)
     each(end_second, jobs_q)
-    each(open_second, jobs_s)
-
-    def project(q_ref):
+
+    def project(q_ref, lo, n):
         def body(yy, carry):
             lanes = pl.ds(pl.multiple_of(yy * QW, QW), QW)
-            qkv[:, lanes] = dot(normin[...], qkv_rows(q_ref, yy)).astype(bf16)
+            qkv[lo:lo + n, lanes] = dot(normin[lo:lo + n, :], qkv_rows(q_ref, yy)).astype(bf16)
             return carry
         lax.fori_loop(0, NY, body, 0)
 
@@ -389,16 +407,6 @@
             return carry
         lax.fori_loop(lo, hi, body, 0)
 
-    dqkv[...] = jnp.zeros((TOK, NY * QW), bf16)
-
-    def own_norms(i, carry):
-        rows = pl.ds(pl.multiple_of(i * 64, 64), 64)
-        f, r = i // 2, pl.ds(pl.multiple_of((i % 2) * 64, 64), 64)
-        nm_t[rows, :], rs_t[rows, :] = norm_stats(mid[f, r, :].astype(f32))
-        nm_s[rows, :], rs_s[rows, :] = norm_stats(inp[f, r, :].astype(f32))
-        return carry
-    lax.fori_loop(0, 4, own_norms, 0)
-
     wait_scatter(mrecv, arecv_sem, 0)
     acc[...] = dot(pr[...], mrecv[...].reshape(TOK, D))
 
@@ -408,9 +416,11 @@
         normin[rows, :] = (normed * (1.0 + mod[4]) + mod[3]).astype(bf16)
         return carry
     lax.fori_loop(0, 4, patch_norm, 0)
+    each(pass_on, jobs_s, 0)
+    each(open_second, jobs_s)
     each(share_wait, jobs_q)
-    project(q_t)
     for b in range(2):
+        project(q_t, 128 * b, 128)
         attend(True, b, b + 1)
         wait_scatter(drecv.at[b], arecv_sem, 1 + b)
         dout[128 * b:128 * b + 128, :] = drecv[b].reshape(128, HEADS * HP)
@@ -430,7 +440,7 @@
         return carry
     lax.fori_loop(0, 4, frame_norm, 0)
     each(share_wait, jobs_s)
-    project(q_s)
+    project(q_s, 0, TOK)
     attend(False)
 
     wait_scatter(rrecv.at[0], arecv_sem, 3)
@@ -514,7 +524,7 @@
             pltpu.VMEM((TOK, D), f32),
             pltpu.VMEM((TOK, 1), f32),
             pltpu.VMEM((TOK, D), f32),
-            dma((2, 8)), dma((2, 8)), dma((8, 12)), dma((8, 12)), dma((5,)), dma((5,)),
+            dma((2, 2, 8)), dma((2, 2, 8)), dma((8, 12)), dma((8, 12)), dma((5,)), dma((5,)),
         ],
         compiler_params=pltpu.CompilerParams(
             collective_id=0, has_side_effects=True, vmem_limit_bytes=56 * 1024 * 1024

time: 130 us -> 129 us (level)
  no operation moved by 1% of the time
where the time goes in v5:
time: 129 us
  Pallas kernels  126 us (98%)
  local copies, waits for them, and re-layouts  1.92 us (1%)
    pallas_call x1, Pallas kernels, per_device(): pl.pallas_call(kernel, out_shape=jax.ShapeDtypeStruct((2, 128, D), bf16),...  126 us

profile of v5, /device:TPU:1, one launch (start us, length us, event | category | flops | bytes accessed | tf_op | source)
XLA Modules:
  0.0 128.7 jit_solution(545040587904121123)
XLA Ops:
  0.7 126.1 %blocks_grad.1 = bf16[2,128,1152]{2,1,0:T(8,128)(2,1)} custom-call(bf16[2,128,1152]{2,1,0:T(8,128)(2,1)} %bitcast.10, bf16[2,128,1152]{2,1,0:T(8,128)(2,1)} %bitcast.11, bf16[2,128,1152]{2,1,0:T(8,128)(2,1)} %bitcast.12, f32[6,1,1152]{2,1,0:T(1,128)} %bitcast.13, s32[1]{0:T(128)S(6)} %copy.11.frames, bf16[27,144]{1,0:T(8,128)(2,1)} %bitcast.14, ...), custom_call_target="tpu_custom_call" | custom-call | tf_op jit(solution)/shard_map/blocks_grad/pallas_call | solution.py:485
  126.7 1.9 %copy.12 = bf16[1,2,128,1152]{3,2,1,0:T(8,128)(2,1)} copy(bf16[1,2,128,1152]{3,2,1,0:T(8,128)(2,1)} %bitcast.9) | data formatting | bytes 1179648

commit v6 on v5

--- a/solution.py
+++ b/solution.py
@@ -208,7 +208,7 @@
     for step in range(8):
         ring_step(0, step)
         ring_step(1, step)
-        send_mid(step, step + 1)
+        send_mid(3 * step, 3 * step + 3)
         lax.fori_loop(2 * step, 2 * step + 2, fill, 0)
         if step == 1:
             for cp in loads[5:]:
@@ -330,18 +330,17 @@
     each(first_step, jobs_o, 0)
     unpack(0, q_t)
     each(first_step, jobs_q, 0)
-    send_mid(8, 20)
+    send_mid(24, 40)
     ring_step(1, 8)
     unpack(1, o_s)
     unpack(1, q_s)
     each(pass_on, jobs_o, 0)
     each(open_second, jobs_o)
-    send_mid(20, 32)
+    send_mid(40, 54)
     each(pass_on, jobs_q, 0)
-    send_mid(32, 44)
+    send_mid(54, 63)
     each(on_second, jobs_o)
     each(open_second, jobs_q)
-    send_mid(44, 63)
     each(end_second, jobs_o)
     each(first_step, jobs_s, 0)
 

time: 129 us -> 131 us (1.016)
  Pallas kernels: 126 us -> 128 us
    pallas_call x1, Pallas kernels: 126 us -> 128 us  [per_device(): pl.pallas_call(kernel, out_shape=jax.ShapeDtypeStruct((2, 128, D), bf16),...]
where the time goes in v6:
time: 131 us
  Pallas kernels  128 us (98%)
  local copies, waits for them, and re-layouts  1.92 us (1%)
    pallas_call x1, Pallas kernels, per_device(): pl.pallas_call(kernel, out_shape=jax.ShapeDtypeStruct((2, 128, D), bf16),...  128 us

profile of v6, /device:TPU:1, one launch (start us, length us, event | category | flops | bytes accessed | tf_op | source)
XLA Modules:
  0.0 130.6 jit_solution(17340362674098633131)
XLA Ops:
  0.7 128.0 %blocks_grad.1 = bf16[2,128,1152]{2,1,0:T(8,128)(2,1)} custom-call(bf16[2,128,1152]{2,1,0:T(8,128)(2,1)} %bitcast.10, bf16[2,128,1152]{2,1,0:T(8,128)(2,1)} %bitcast.11, bf16[2,128,1152]{2,1,0:T(8,128)(2,1)} %bitcast.12, f32[6,1,1152]{2,1,0:T(1,128)} %bitcast.13, s32[1]{0:T(128)S(6)} %copy.11.frames, bf16[27,144]{1,0:T(8,128)(2,1)} %bitcast.14, ...), custom_call_target="tpu_custom_call" | custom-call | tf_op jit(solution)/shard_map/blocks_grad/pallas_call | solution.py:484
  128.7 1.9 %copy.12 = bf16[1,2,128,1152]{3,2,1,0:T(8,128)(2,1)} copy(bf16[1,2,128,1152]{3,2,1,0:T(8,128)(2,1)} %bitcast.9) | data formatting | bytes 1179648

commit v7 on v6

--- a/solution.py
+++ b/solution.py
@@ -54,10 +54,10 @@
 def kernel(
     inp_hbm, mid_hbm, cot_hbm, mod_hbm, frames, qkv_s_hbm, out_s_hbm, qkv_t_hbm, out_t_hbm, result,
     inp, mid, cot, mod, qkv_s, out_s, qkv_t, out_t, load_sem,
-    zbuf, eq, eo, q_t, o_t, q_s, o_s,
+    z_qt, z_s, z_ot, eq, eo, q_t, o_t, q_s, o_s,
     msend, mrecv, dsend, drecv, rsend, rrecv,
     pm, pr, back, normin, qkv, dqkv, dout, probs, acc, nm_t, rs_t, nm_s, rs_s, dmid,
-    zsend_sem, zrecv_sem, jsend_sem, jrecv_sem, asend_sem, arecv_sem,
+    osem, zsend_sem, zrecv_sem, jsend_sem, jrecv_sem, asend_sem, arecv_sem,
 ):
     dp = lax.axis_index("dp")
     s = lax.axis_index("seq")
@@ -109,26 +109,24 @@
     pl.semaphore_signal(barrier, inc=1, device_id={"dp": x * 2 + other})
     each_peer(lambda to: pl.semaphore_signal(barrier, inc=1, device_id={"seq": to}))
 
-    def pack(qkv_ref, out_ref):
-        q, o = qkv_ref[...], out_ref[...]
-
-        def place(rows, g):
-            hit = iota((rows, 128), 1) == iota((rows, 128), 0) + 32 * g
-            return jnp.where(hit, 1.0, 0.0).astype(bf16)
-
-        q0 = dot(q, place(27, 0), TN)[0:64]
-        q1 = dot(q, place(27, 1), TN)[64:128]
-        q2 = dot(q, place(27, 2), TN)[128:144]
-        o2 = dot(o, place(18, 2), TN)[0:48]
-        o3 = dot(o, place(18, 3), TN)[48:72]
-        full = q0 + q1 + jnp.concatenate([q2, o2], 0)
-        full = full + jnp.concatenate([o3, jnp.zeros((40, 128), f32)], 0)
-        return full.astype(bf16)
+    def pack(ref, group, lanes):
+        w = ref[...]
+        n, rows = w.shape
+        total = None
+        for g in range(-(-rows // group)):
+            hit = iota((n, 128), 1) == iota((n, 128), 0) + lanes * g
+            part = dot(w, jnp.where(hit, 1.0, 0.0).astype(bf16), TN)[group * g:group * (g + 1)]
+            if part.shape[0] < group:
+                part = jnp.concatenate([part, jnp.zeros((group - part.shape[0], 128), f32)], 0)
+            total = part if total is None else total + part
+        return total.astype(bf16)
 
     for cp in loads[:4]:
         cp.wait()
-    zbuf[z, 0] = pack(qkv_t, out_t)
-    zbuf[z, 1] = pack(qkv_s, out_s)
+    z_ot[z] = pack(out_t, 16, 24)
+    z_qt[z] = pack(qkv_t, 48, 32)
+    z_s[z, 0:48] = pack(qkv_s, 48, 32)
+    z_s[z, 48:64] = pack(out_s, 16, 24)
 
     ri, ci = iota((TOK, TOK), 0), iota((TOK, TOK), 1)
     pm[...] = jnp.where(ci == (ri & 1) * 128 + (ri >> 2) * 2 + ((ri >> 1) & 1), 1.0, 0.0).astype(bf16)
@@ -147,7 +145,7 @@
 
     def zcopy(kind, block, way, step):
         to = lax.rem(z + 1, NZ) if way == 0 else lax.rem(z + NZ - 1, NZ)
-        ref = zbuf.at[block, kind]
+        ref = (z_qt, z_s)[kind].at[block]
         return pltpu.make_async_remote_copy(
             src_ref=ref, dst_ref=ref,
             send_sem=zsend_sem.at[kind, way, step], recv_sem=zrecv_sem.at[kind, way, step],
@@ -183,14 +181,19 @@
         part = ref.at[pl.ds(0, NSEQ - 1)]
         pltpu.make_async_copy(part, part, sem.at[k]).wait()
 
-    def fill(zz, carry):
-        lane = iota((224, QW), 0) - 96
-        live = (lane >= 0) & (lane < 27)
-        hit = live & (iota((224, QW), 1) == lane + 27 * zz)
+    def fill_q(zz, carry):
+        lane, col = iota((128, QW), 0), iota((128, QW), 1)
+        at = lane & 31
+        hit = (at < 27) & (lane < 96) & (col == at + 27 * zz)
         eq[zz] = jnp.where(hit, 1.0, 0.0).astype(bf16)
-        lane = iota((224, OW), 0) - 96
-        live = (lane >= 0) & (lane < 18)
-        hit = live & (iota((224, OW), 1) == lane + 18 * zz + 32 * y)
+        return carry
+
+    def fill_o(zz, carry):
+        lane, col = iota((128, OW), 0), iota((128, OW), 1)
+        at = lane
+        for g in range(1, 5):
+            at = jnp.where(lane >= 24 * g, lane - 24 * g, at)
+        hit = (at < 18) & (col == at + 18 * zz + 32 * y)
         eo[zz] = jnp.where(hit, 1.0, 0.0).astype(bf16)
         return carry
 
@@ -205,33 +208,33 @@
         cell = iota((128, 1), 0) * 0 + (2 * s + f)
         return jnp.where(cell < frames[0], cot[f].astype(f32), 0.0)
 
-    for step in range(8):
-        ring_step(0, step)
-        ring_step(1, step)
-        send_mid(3 * step, 3 * step + 3)
-        lax.fori_loop(2 * step, 2 * step + 2, fill, 0)
-        if step == 1:
-            for cp in loads[5:]:
-                cp.wait()
-        if step in (2, 3):
-            f = step - 2
-            normin[f * 128:(f + 1) * 128, :] = (live_cot(f) * mod[5]).astype(bf16)
-        if step > 3:
-            lax.fori_loop(step - 4, step - 3, own_norms, 0)
-    ring_step(0, 8)
-
-    def unpack(kind, ref):
-        whole = jnp.concatenate([zbuf[i, kind] for i in range(NZ)], 1)
-        table = eo if ref is o_t or ref is o_s else eq
-
-        def pick(g):
-            lo = 96 - 32 * g
-            return dot(whole, table[:, lo:lo + 128, :].reshape(NZ * 128, -1)).astype(bf16)
-
-        if table is eo:
-            ref[y, c, x] = jnp.concatenate([pick(2)[16:64], pick(3)[0:32]], 0)
-        else:
-            ref[y, c, x] = jnp.concatenate([pick(0), pick(1), pick(2)[0:16]], 0)
+    def whole_of(ref, lo, hi):
+        return jnp.concatenate([ref[i, lo:hi] for i in range(NZ)], 1)
+
+    def unpack(whole, table, group, lanes, count):
+        lane = iota(whole.shape, 1) & 127
+        parts = []
+        for g in range(count):
+            live = (lane >= lanes * g) & (lane < lanes * (g + 1))
+            parts.append(jnp.where(live, whole, jnp.zeros_like(whole)))
+        lhs = jnp.concatenate(parts, 0)
+        return dot(lhs, table[...].reshape(NZ * 128, -1)).astype(bf16)
+
+    def unpack_q(whole):
+        return unpack(whole, eq, 48, 32, 3)
+
+    def unpack_o(whole):
+        return unpack(whole, eo, 16, 24, 5)
+
+    def o_to(to):
+        pltpu.make_async_remote_copy(
+            src_ref=z_ot.at[z], dst_ref=z_ot.at[z], send_sem=osem.at[0], recv_sem=osem.at[1],
+            device_id=seq_dev(y, to),
+        ).start()
+
+    def o_wait(k):
+        part = z_ot.at[pl.ds(0, NZ - 1)]
+        pltpu.make_async_copy(part, part, osem.at[k]).wait()
 
     jobs_t = [
         (0, o_t, "y", 0, 32, 16), (1, o_t, "x", 32, 48, 32),
@@ -326,23 +329,40 @@
             f(job, *args)
 
     jobs_o, jobs_q = jobs_t[:2], jobs_t[2:]
-    unpack(0, o_t)
-    each(first_step, jobs_o, 0)
-    unpack(0, q_t)
+
+    for m in range(8, 0, -1):
+        o_to(lax.rem(z + m, NZ))
+        if m < 8:
+            o_to(lax.rem(z + NZ - m, NZ))
+    for step in range(8):
+        ring_step(0, step)
+        ring_step(1, step)
+        send_mid(2 * step, 2 * step + 2)
+        if step == 0:
+            lax.fori_loop(0, NZ, fill_o, 0)
+        else:
+            lax.fori_loop(3 * step - 3, min(3 * step, NZ), fill_q, 0)
+        if step == 1:
+            for cp in loads[5:]:
+                cp.wait()
+        if step == 2:
+            o_wait(1)
+            o_t[y, c, x] = unpack_o(whole_of(z_ot, 0, 16))
+            each(first_step, jobs_o, 0)
+        if step in (3, 6):
+            f = step // 3 - 1
+            normin[f * 128:(f + 1) * 128, :] = (live_cot(f) * mod[5]).astype(bf16)
+        if step == 4:
+            each(pass_on, jobs_o, 0)
+        if step == 5:
+            each(open_second, jobs_o)
+        if step == 7:
+            each(on_second, jobs_o)
+    ring_step(0, 8)
+    q_t[y, c, x] = unpack_q(whole_of(z_qt, 0, 48))
     each(first_step, jobs_q, 0)
-    send_mid(24, 40)
-    ring_step(1, 8)
-    unpack(1, o_s)
-    unpack(1, q_s)
-    each(pass_on, jobs_o, 0)
-    each(open_second, jobs_o)
-    send_mid(40, 54)
-    each(pass_on, jobs_q, 0)
-    send_mid(54, 63)
-    each(on_second, jobs_o)
-    each(open_second, jobs_q)
+    send_mid(16, 63)
     each(end_second, jobs_o)
-    each(first_step, jobs_s, 0)
 
     each(share_wait, jobs_o)
     dout[...] = out_back(normin, o_t)
@@ -352,6 +372,13 @@
         scatter(dsend.at[b], drecv.at[b], 1 + b)
         drecv[b, s] = dsend[b, s]
     mrecv[s] = msend[s]
+    each(pass_on, jobs_q, 0)
+    ring_step(1, 8)
+    o_s[y, c, x] = unpack_o(whole_of(z_s, 48, 64))
+    q_s[y, c, x] = unpack_q(whole_of(z_s, 0, 48))
+    each(open_second, jobs_q)
+    each(first_step, jobs_s, 0)
+    lax.fori_loop(0, 4, own_norms, 0)
     each(on_second, jobs_q)
     each(end_second, jobs_q)
 
@@ -442,6 +469,13 @@
     project(q_s, 0, TOK)
     attend(False)
 
+    for cp in pending:
+        cp.wait_send()
+    o_wait(0)
+    wait_scatter(msend, asend_sem, 0)
+    for b in range(2):
+        wait_scatter(dsend.at[b], asend_sem, 1 + b)
+
     wait_scatter(rrecv.at[0], arecv_sem, 3)
     acc[...] = dot(back[:, 0:128], rrecv[0].reshape(128, D))
     wait_scatter(rrecv.at[1], arecv_sem, 4)
@@ -470,11 +504,7 @@
         return carry
     lax.fori_loop(0, 4, last_grad, 0)
 
-    for cp in pending:
-        cp.wait_send()
-    wait_scatter(msend, asend_sem, 0)
     for b in range(2):
-        wait_scatter(dsend.at[b], asend_sem, 1 + b)
         wait_scatter(rsend.at[b], asend_sem, 3 + b)
 
 
@@ -496,9 +526,11 @@
             pltpu.VMEM((27, 144), bf16),
             pltpu.VMEM((18, 72), bf16),
             dma((8,)),
-            pltpu.VMEM((NZ, 2, 64, 128), bf16),
-            pltpu.VMEM((NZ, 224, QW), bf16),
-            pltpu.VMEM((NZ, 224, OW), bf16),
+            pltpu.VMEM((NZ, 48, 128), bf16),
+            pltpu.VMEM((NZ, 64, 128), bf16),
+            pltpu.VMEM((NZ, 16, 128), bf16),
+            pltpu.VMEM((NZ, 128, QW), bf16),
+            pltpu.VMEM((NZ, 128, OW), bf16),
             pltpu.VMEM((NY, 2, NX, 144, QW), bf16),
             pltpu.VMEM((NY, 2, NX, HP, OW), bf16),
             pltpu.VMEM((NY, 2, NX, 144, QW), bf16),
@@ -523,7 +555,7 @@
             pltpu.VMEM((TOK, D), f32),
             pltpu.VMEM((TOK, 1), f32),
             pltpu.VMEM((TOK, D), f32),
-            dma((2, 2, 8)), dma((2, 2, 8)), dma((8, 12)), dma((8, 12)), dma((5,)), dma((5,)),
+            dma((2,)), dma((2, 2, 8)), dma((2, 2, 8)), dma((8, 12)), dma((8, 12)), dma((5,)), dma((5,)),
         ],
         compiler_params=pltpu.CompilerParams(
             collective_id=0, has_side_effects=True, vmem_limit_bytes=56 * 1024 * 1024

time: 131 us -> 130 us (level)
  no operation moved by 1% of the time
where the time goes in v7:
time: 130 us
  Pallas kernels  127 us (98%)
  local copies, waits for them, and re-layouts  1.92 us (1%)
    pallas_call x1, Pallas kernels, per_device(): pl.pallas_call(kernel, out_shape=jax.ShapeDtypeStruct((2, 128, D), bf16),...  127 us

profile of v7, /device:TPU:1, one launch (start us, length us, event | category | flops | bytes accessed | tf_op | source)
XLA Modules:
  0.0 129.8 jit_solution(2434459888864814103)
XLA Ops:
  0.7 127.2 %blocks_grad.1 = bf16[2,128,1152]{2,1,0:T(8,128)(2,1)} custom-call(bf16[2,128,1152]{2,1,0:T(8,128)(2,1)} %bitcast.10, bf16[2,128,1152]{2,1,0:T(8,128)(2,1)} %bitcast.11, bf16[2,128,1152]{2,1,0:T(8,128)(2,1)} %bitcast.12, f32[6,1,1152]{2,1,0:T(1,128)} %bitcast.13, s32[1]{0:T(128)S(6)} %copy.11.frames, bf16[27,144]{1,0:T(8,128)(2,1)} %bitcast.14, ...), custom_call_target="tpu_custom_call" | custom-call | tf_op jit(solution)/shard_map/blocks_grad/pallas_call | solution.py:514
  127.9 1.9 %copy.12 = bf16[1,2,128,1152]{3,2,1,0:T(8,128)(2,1)} copy(bf16[1,2,128,1152]{3,2,1,0:T(8,128)(2,1)} %bitcast.9) | data formatting | bytes 1179648

commit v8 on v7

--- a/solution.py
+++ b/solution.py
@@ -143,23 +143,34 @@
 
     pl.semaphore_wait(barrier, NSEQ - 1 + 3)
 
-    def zcopy(kind, block, way, step):
-        to = lax.rem(z + 1, NZ) if way == 0 else lax.rem(z + NZ - 1, NZ)
+    def zcopy(kind, way, dist, block):
+        hop = min(dist, 2)
+        to = lax.rem(z + hop, NZ) if way == 0 else lax.rem(z + NZ - hop, NZ)
         ref = (z_qt, z_s)[kind].at[block]
         return pltpu.make_async_remote_copy(
             src_ref=ref, dst_ref=ref,
-            send_sem=zsend_sem.at[kind, way, step], recv_sem=zrecv_sem.at[kind, way, step],
+            send_sem=zsend_sem.at[kind, way, dist - 1], recv_sem=zrecv_sem.at[kind, way, dist - 1],
             device_id=seq_dev(y, to),
         )
 
+    def ring_send(kind, way, dist, block):
+        cp = zcopy(kind, way, dist, block)
+        cp.start()
+        pending.append(cp)
+
     def ring_step(kind, step):
-        for way, block in ((0, lax.rem(z + NZ - step, NZ)), (1, lax.rem(z + step, NZ))):
-            if step > 0 and not (way == 1 and step == 8):
-                zcopy(kind, block, way, step - 1).wait_recv()
-            if step < 8 - way:
-                cp = zcopy(kind, block, way, step)
-                cp.start()
-                pending.append(cp)
+        if step == 0:
+            for dist in (1, 2):
+                for way in (0, 1):
+                    ring_send(kind, way, dist, z)
+            return
+        for dist in (2 * step - 1, 2 * step):
+            for way, block in ((0, lax.rem(z + NZ - dist, NZ)), (1, lax.rem(z + dist, NZ))):
+                if dist > 8 - way:
+                    continue
+                zcopy(kind, way, dist, block).wait_recv()
+                if dist + 2 <= 8 - way:
+                    ring_send(kind, way, dist + 2, block)
 
     def send_to(src, dst, k, to):
         pltpu.make_async_remote_copy(
@@ -245,25 +256,29 @@
         (6, q_s, "y", 0, 80, 48), (7, q_s, "x", 80, 64, 32),
     ]
 
-    def view(job, phase, rel, half, core):
+    def view(job, phase, rel, half, core, elem):
         _, ref, first, r, n, m = job
         lo, size = {"all": (r, n), "a": (r, m), "b": (r + m, n - m)}[half]
         rows = pl.ds(lo, size)
-        axis = first if phase == 0 else ("x" if first == "y" else "y")
-        if axis == "x":
-            return ref.at[y if phase == 0 else slice(None), core, (x + rel) % NX, rows]
-        return ref.at[(y + rel) % NY, core, x if phase == 0 else slice(None), rows]
-
-    def hop(job, phase, rel, half, way, slot):
+        along = {"x": x, "y": y}
+        if phase == 0:
+            along[first] = lax.rem(along[first] + rel, NX)
+        else:
+            second = "x" if first == "y" else "y"
+            along[second] = lax.rem(along[second] + rel, NX)
+            along[first] = slice(None) if elem is None else lax.rem(along[first] + elem, NX)
+        return ref.at[along["y"], core, along["x"], rows]
+
+    def hop(job, phase, rel, half, way, slot, elem=0):
         first = job[2]
         axis = first if phase == 0 else ("x" if first == "y" else "y")
         step = 1 if way == 0 else 3
-        dev = x_dev((x + step) % NX) if axis == "x" else seq_dev((y + step) % NY, z)
-        ref = view(job, phase, rel, half, c)
+        dev = x_dev(lax.rem(x + step, NX)) if axis == "x" else seq_dev(lax.rem(y + step, NY), z)
+        ref = view(job, phase, rel, half, c, elem)
+        at = slot if phase == 0 else 4 + 4 * elem + slot
         return pltpu.make_async_remote_copy(
             src_ref=ref, dst_ref=ref,
-            send_sem=jsend_sem.at[job[0], phase * 4 + slot],
-            recv_sem=jrecv_sem.at[job[0], phase * 4 + slot],
+            send_sem=jsend_sem.at[job[0], at], recv_sem=jrecv_sem.at[job[0], at],
             device_id=dev,
         )
 
@@ -271,25 +286,27 @@
         cp.start()
         pending.append(cp)
 
-    def first_step(job, phase):
-        go(hop(job, phase, 0, "all", 0, 0))
-        go(hop(job, phase, 0, "all", 1, 1))
-
-    def pass_on(job, phase):
-        hop(job, phase, 3, "all", 0, 0).wait_recv()
-        go(hop(job, phase, 3, "a", 0, 2))
-        hop(job, phase, 1, "all", 1, 1).wait_recv()
-        go(hop(job, phase, 1, "b", 1, 3))
-
-    def last_step(job, phase):
-        hop(job, phase, 2, "a", 0, 2).wait_recv()
-        hop(job, phase, 2, "b", 1, 3).wait_recv()
+    def first_step(job, phase, elem=0):
+        go(hop(job, phase, 0, "all", 0, 0, elem))
+        go(hop(job, phase, 0, "all", 1, 1, elem))
+
+    def pass_left(job, phase, elem=0):
+        hop(job, phase, 3, "all", 0, 0, elem).wait_recv()
+        go(hop(job, phase, 3, "a", 0, 2, elem))
+
+    def pass_right(job, phase, elem=0):
+        hop(job, phase, 1, "all", 1, 1, elem).wait_recv()
+        go(hop(job, phase, 1, "b", 1, 3, elem))
+
+    def last_step(job, phase, elem=0):
+        hop(job, phase, 2, "a", 0, 2, elem).wait_recv()
+        hop(job, phase, 2, "b", 1, 3, elem).wait_recv()
 
     def share(job, rel, core):
-        ref = view(job, 1, rel, "all", core)
+        ref = view(job, 1, rel, "all", core, None)
         return pltpu.make_async_remote_copy(
             src_ref=ref, dst_ref=ref,
-            send_sem=jsend_sem.at[job[0], 8 + rel], recv_sem=jrecv_sem.at[job[0], 8 + rel],
+            send_sem=jsend_sem.at[job[0], 20 + rel], recv_sem=jrecv_sem.at[job[0], 20 + rel],
             device_id={"dp": x * 2 + other},
         )
 
@@ -310,18 +327,33 @@
             total = term if total is None else total + term
         return total.astype(bf16)
 
-    def open_second(job):
+    def begin(job):
+        first_step(job, 0)
+        first_step(job, 1, 0)
+
+    def second(job):
+        pass_left(job, 0)
+        first_step(job, 1, 3)
+        pass_right(job, 0)
+        first_step(job, 1, 1)
+
+    def third(job):
         last_step(job, 0)
-        first_step(job, 1)
+        first_step(job, 1, 2)
+        pass_left(job, 1, 0)
+        pass_right(job, 1, 0)
         go(share(job, 0, c))
 
-    def on_second(job):
-        pass_on(job, 1)
+    def fourth(job):
+        for elem in (3, 1, 2):
+            pass_left(job, 1, elem)
+            pass_right(job, 1, elem)
         go(share(job, 3, c))
         go(share(job, 1, c))
 
-    def end_second(job):
-        last_step(job, 1)
+    def fifth(job):
+        for elem in (0, 3, 1, 2):
+            last_step(job, 1, elem)
         go(share(job, 2, c))
 
     def each(f, jobs, *args):
@@ -334,35 +366,41 @@
         o_to(lax.rem(z + m, NZ))
         if m < 8:
             o_to(lax.rem(z + NZ - m, NZ))
-    for step in range(8):
-        ring_step(0, step)
-        ring_step(1, step)
-        send_mid(2 * step, 2 * step + 2)
-        if step == 0:
-            lax.fori_loop(0, NZ, fill_o, 0)
-        else:
-            lax.fori_loop(3 * step - 3, min(3 * step, NZ), fill_q, 0)
-        if step == 1:
-            for cp in loads[5:]:
-                cp.wait()
-        if step == 2:
-            o_wait(1)
-            o_t[y, c, x] = unpack_o(whole_of(z_ot, 0, 16))
-            each(first_step, jobs_o, 0)
-        if step in (3, 6):
-            f = step // 3 - 1
-            normin[f * 128:(f + 1) * 128, :] = (live_cot(f) * mod[5]).astype(bf16)
-        if step == 4:
-            each(pass_on, jobs_o, 0)
-        if step == 5:
-            each(open_second, jobs_o)
-        if step == 7:
-            each(on_second, jobs_o)
-    ring_step(0, 8)
+    ring_step(0, 0)
+    ring_step(1, 0)
+    send_mid(0, 8)
+    lax.fori_loop(0, NZ, fill_o, 0)
+    for cp in loads[5:]:
+        cp.wait()
+    ring_step(0, 1)
+    ring_step(1, 1)
+    send_mid(8, 12)
+    o_wait(1)
+    o_t[y, c, x] = unpack_o(whole_of(z_ot, 0, 16))
+    each(begin, jobs_o)
+    lax.fori_loop(0, NZ, fill_q, 0)
+    ring_step(0, 2)
+    ring_step(1, 2)
+    send_mid(12, 16)
+    each(second, jobs_o)
+    ring_step(0, 3)
+    ring_step(1, 3)
+    send_mid(16, 20)
+    for f in range(2):
+        normin[f * 128:(f + 1) * 128, :] = (live_cot(f) * mod[5]).astype(bf16)
+    ring_step(0, 4)
     q_t[y, c, x] = unpack_q(whole_of(z_qt, 0, 48))
-    each(first_step, jobs_q, 0)
-    send_mid(16, 63)
-    each(end_second, jobs_o)
+    each(begin, jobs_q)
+    each(third, jobs_o)
+    send_mid(20, 40)
+    ring_step(1, 4)
+    o_s[y, c, x] = unpack_o(whole_of(z_s, 48, 64))
+    q_s[y, c, x] = unpack_q(whole_of(z_s, 0, 48))
+    each(second, jobs_q)
+    send_mid(40, 63)
+    each(fourth, jobs_o)
+    each(third, jobs_q)
+    each(fifth, jobs_o)
 
     each(share_wait, jobs_o)
     dout[...] = out_back(normin, o_t)
@@ -372,15 +410,10 @@
         scatter(dsend.at[b], drecv.at[b], 1 + b)
         drecv[b, s] = dsend[b, s]
     mrecv[s] = msend[s]
-    each(pass_on, jobs_q, 0)
-    ring_step(1, 8)
-    o_s[y, c, x] = unpack_o(whole_of(z_s, 48, 64))
-    q_s[y, c, x] = unpack_q(whole_of(z_s, 0, 48))
-    each(open_second, jobs_q)
-    each(first_step, jobs_s, 0)
+    each(begin, jobs_s)
     lax.fori_loop(0, 4, own_norms, 0)
-    each(on_second, jobs_q)
-    each(end_second, jobs_q)
+    each(fourth, jobs_q)
+    each(fifth, jobs_q)
 
     def project(q_ref, lo, n):
         def body(yy, carry):
@@ -442,11 +475,12 @@
         normin[rows, :] = (normed * (1.0 + mod[4]) + mod[3]).astype(bf16)
         return carry
     lax.fori_loop(0, 4, patch_norm, 0)
-    each(pass_on, jobs_s, 0)
-    each(open_second, jobs_s)
+    each(second, jobs_s)
     each(share_wait, jobs_q)
     for b in range(2):
         project(q_t, 128 * b, 128)
+        if b == 0:
+            each(third, jobs_s)
         attend(True, b, b + 1)
         wait_scatter(drecv.at[b], arecv_sem, 1 + b)
         dout[128 * b:128 * b + 128, :] = drecv[b].reshape(128, HEADS * HP)
@@ -456,9 +490,9 @@
         scatter(rsend.at[b], rrecv.at[b], 3 + b)
         rrecv[b, s] = rsend[b, s]
         if b == 0:
-            each(on_second, jobs_s)
-
-    each(end_second, jobs_s)
+            each(fourth, jobs_s)
+
+    each(fifth, jobs_s)
 
     def frame_norm(i, carry):
         rows = pl.ds(pl.multiple_of(i * 64, 64), 64)
@@ -555,7 +589,7 @@
             pltpu.VMEM((TOK, D), f32),
             pltpu.VMEM((TOK, 1), f32),
             pltpu.VMEM((TOK, D), f32),
-            dma((2,)), dma((2, 2, 8)), dma((2, 2, 8)), dma((8, 12)), dma((8, 12)), dma((5,)), dma((5,)),
+            dma((2,)), dma((2, 2, 8)), dma((2, 2, 8)), dma((8, 24)), dma((8, 24)), dma((5,)), dma((5,)),
         ],
         compiler_params=pltpu.CompilerParams(
             collective_id=0, has_side_effects=True, vmem_limit_bytes=56 * 1024 * 1024

time: 130 us -> 134 us (1.031)
  Pallas kernels: 127 us -> 131 us
    pallas_call x1, Pallas kernels: 127 us -> 131 us  [per_device(): pl.pallas_call(kernel, out_shape=jax.ShapeDtypeStruct((2, 128, D), bf16),...]
where the time goes in v8:
time: 134 us
  Pallas kernels  131 us (98%)
  local copies, waits for them, and re-layouts  1.92 us (1%)
    pallas_call x1, Pallas kernels, per_device(): pl.pallas_call(kernel, out_shape=jax.ShapeDtypeStruct((2, 128, D), bf16),...  131 us

profile of v8, /device:TPU:1, one launch (start us, length us, event | category | flops | bytes accessed | tf_op | source)
XLA Modules:
  0.0 134.0 jit_solution(9203293306022429996)
XLA Ops:
  0.7 131.4 %blocks_grad.1 = bf16[2,128,1152]{2,1,0:T(8,128)(2,1)} custom-call(bf16[2,128,1152]{2,1,0:T(8,128)(2,1)} %bitcast.10, bf16[2,128,1152]{2,1,0:T(8,128)(2,1)} %bitcast.11, bf16[2,128,1152]{2,1,0:T(8,128)(2,1)} %bitcast.12, f32[6,1,1152]{2,1,0:T(1,128)} %bitcast.13, s32[1]{0:T(128)S(6)} %copy.11.frames, bf16[27,144]{1,0:T(8,128)(2,1)} %bitcast.14, ...), custom_call_target="tpu_custom_call" | custom-call | tf_op jit(solution)/shard_map/blocks_grad/pallas_call | solution.py:548
  132.0 1.9 %copy.12 = bf16[1,2,128,1152]{3,2,1,0:T(8,128)(2,1)} copy(bf16[1,2,128,1152]{3,2,1,0:T(8,128)(2,1)} %bitcast.9) | data formatting | bytes 1179648

commit v9 on v7

--- a/solution.py
+++ b/solution.py
@@ -54,10 +54,10 @@
 def kernel(
     inp_hbm, mid_hbm, cot_hbm, mod_hbm, frames, qkv_s_hbm, out_s_hbm, qkv_t_hbm, out_t_hbm, result,
     inp, mid, cot, mod, qkv_s, out_s, qkv_t, out_t, load_sem,
-    z_qt, z_s, z_ot, eq, eo, q_t, o_t, q_s, o_s,
+    z_t, z_s, eq, eo, q_t, o_t, q_s, o_s,
     msend, mrecv, dsend, drecv, rsend, rrecv,
     pm, pr, back, normin, qkv, dqkv, dout, probs, acc, nm_t, rs_t, nm_s, rs_s, dmid,
-    osem, zsend_sem, zrecv_sem, jsend_sem, jrecv_sem, asend_sem, arecv_sem,
+    zsend_sem, zrecv_sem, jsend_sem, jrecv_sem, asend_sem, arecv_sem,
 ):
     dp = lax.axis_index("dp")
     s = lax.axis_index("seq")
@@ -123,29 +123,15 @@
 
     for cp in loads[:4]:
         cp.wait()
-    z_ot[z] = pack(out_t, 16, 24)
-    z_qt[z] = pack(qkv_t, 48, 32)
-    z_s[z, 0:48] = pack(qkv_s, 48, 32)
-    z_s[z, 48:64] = pack(out_s, 16, 24)
-
-    ri, ci = iota((TOK, TOK), 0), iota((TOK, TOK), 1)
-    pm[...] = jnp.where(ci == (ri & 1) * 128 + (ri >> 2) * 2 + ((ri >> 1) & 1), 1.0, 0.0).astype(bf16)
-    pr[...] = jnp.where(
-        ci == ((ri & 127) >> 1) * 4 + (ri >> 7) * 2 + (ri & 1), 1.0, 0.0
-    ).astype(bf16)
-
-    back[...] = jnp.where(
-        ci == (ri & 1) * 128 + ((ri & 127) >> 1) * 2 + (ri >> 7), 1.0, 0.0
-    ).astype(bf16)
-    dqkv[...] = jnp.zeros((TOK, NY * QW), bf16)
-    loads[4].wait()
-    msend[...] = dot(pm[...], mid[...].reshape(TOK, D)).astype(bf16).reshape(NSEQ, 4, D)
+    for ref, q, o in ((z_t, qkv_t, out_t), (z_s, qkv_s, out_s)):
+        ref[z, 0:48] = pack(q, 48, 32)
+        ref[z, 48:64] = pack(o, 16, 24)
 
     pl.semaphore_wait(barrier, NSEQ - 1 + 3)
 
     def zcopy(kind, block, way, step):
         to = lax.rem(z + 1, NZ) if way == 0 else lax.rem(z + NZ - 1, NZ)
-        ref = (z_qt, z_s)[kind].at[block]
+        ref = (z_t, z_s)[kind].at[block]
         return pltpu.make_async_remote_copy(
             src_ref=ref, dst_ref=ref,
             send_sem=zsend_sem.at[kind, way, step], recv_sem=zrecv_sem.at[kind, way, step],
@@ -168,6 +154,17 @@
             device_id={"seq": to},
         ).start()
 
+    def send_pair(src, dst, k, to):
+        pltpu.make_async_remote_copy(
+            src_ref=src.at[:, to], dst_ref=dst.at[:, s],
+            send_sem=asend_sem.at[k], recv_sem=arecv_sem.at[k],
+            device_id={"seq": to},
+        ).start()
+
+    def wait_pairs(ref, sem, k):
+        part = ref.at[:, pl.ds(0, NSEQ - 1)]
+        pltpu.make_async_copy(part, part, sem.at[k]).wait()
+
     def scatter(src, dst, k):
         each_peer(lambda to: send_to(src, dst, k, to))
 
@@ -226,24 +223,9 @@
     def unpack_o(whole):
         return unpack(whole, eo, 16, 24, 5)
 
-    def o_to(to):
-        pltpu.make_async_remote_copy(
-            src_ref=z_ot.at[z], dst_ref=z_ot.at[z], send_sem=osem.at[0], recv_sem=osem.at[1],
-            device_id=seq_dev(y, to),
-        ).start()
-
-    def o_wait(k):
-        part = z_ot.at[pl.ds(0, NZ - 1)]
-        pltpu.make_async_copy(part, part, osem.at[k]).wait()
-
-    jobs_t = [
-        (0, o_t, "y", 0, 32, 16), (1, o_t, "x", 32, 48, 32),
-        (2, q_t, "y", 0, 80, 48), (3, q_t, "x", 80, 64, 32),
-    ]
-    jobs_s = [
-        (4, o_s, "y", 0, 32, 16), (5, o_s, "x", 32, 48, 32),
-        (6, q_s, "y", 0, 80, 48), (7, q_s, "x", 80, 64, 32),
-    ]
+    jobs_o = [(0, o_t, "y", 0, 80, 48)]
+    jobs_q = [(1, q_t, "x", 0, 144, 80)]
+    jobs_s = [(2, o_s, "x", 0, 80, 48), (3, q_s, "y", 0, 144, 80)]
 
     def view(job, phase, rel, half, core):
         _, ref, first, r, n, m = job
@@ -328,40 +310,54 @@
         for job in jobs:
             f(job, *args)
 
-    jobs_o, jobs_q = jobs_t[:2], jobs_t[2:]
-
-    for m in range(8, 0, -1):
-        o_to(lax.rem(z + m, NZ))
-        if m < 8:
-            o_to(lax.rem(z + NZ - m, NZ))
+    ring_step(0, 0)
+    ring_step(1, 0)
+    ri, ci = iota((TOK, TOK), 0), iota((TOK, TOK), 1)
+    pm[...] = jnp.where(ci == (ri & 1) * 128 + (ri >> 2) * 2 + ((ri >> 1) & 1), 1.0, 0.0).astype(bf16)
+    pr[...] = jnp.where(
+        ci == ((ri & 127) >> 1) * 4 + (ri >> 7) * 2 + (ri & 1), 1.0, 0.0
+    ).astype(bf16)
+
+    back[...] = jnp.where(
+        ci == (ri & 1) * 128 + ((ri & 127) >> 1) * 2 + (ri >> 7), 1.0, 0.0
+    ).astype(bf16)
+    dqkv[...] = jnp.zeros((TOK, NY * QW), bf16)
+    loads[4].wait()
+    msend[...] = dot(pm[...], mid[...].reshape(TOK, D)).astype(bf16).reshape(NSEQ, 4, D)
+
     for step in range(8):
-        ring_step(0, step)
-        ring_step(1, step)
+        if step > 0:
+            ring_step(0, step)
+            ring_step(1, step)
         send_mid(2 * step, 2 * step + 2)
-        if step == 0:
-            lax.fori_loop(0, NZ, fill_o, 0)
-        else:
-            lax.fori_loop(3 * step - 3, min(3 * step, NZ), fill_q, 0)
+        lax.fori_loop(2 * step, 2 * step + 2, fill_o, 0)
+        lax.fori_loop(2 * step, 2 * step + 2, fill_q, 0)
         if step == 1:
             for cp in loads[5:]:
                 cp.wait()
-        if step == 2:
-            o_wait(1)
-            o_t[y, c, x] = unpack_o(whole_of(z_ot, 0, 16))
-            each(first_step, jobs_o, 0)
-        if step in (3, 6):
-            f = step // 3 - 1
+        if step in (2, 3):
+            f = step - 2
             normin[f * 128:(f + 1) * 128, :] = (live_cot(f) * mod[5]).astype(bf16)
-        if step == 4:
-            each(pass_on, jobs_o, 0)
-        if step == 5:
-            each(open_second, jobs_o)
-        if step == 7:
-            each(on_second, jobs_o)
+        if step > 3:
+            lax.fori_loop(step - 4, step - 3, own_norms, 0)
     ring_step(0, 8)
-    q_t[y, c, x] = unpack_q(whole_of(z_qt, 0, 48))
+    o_t[y, c, x] = unpack_o(whole_of(z_t, 48, 64))
+    each(first_step, jobs_o, 0)
+    q_t[y, c, x] = unpack_q(whole_of(z_t, 0, 48))
     each(first_step, jobs_q, 0)
-    send_mid(16, 63)
+    send_mid(16, 28)
+    ring_step(1, 8)
+    each(pass_on, jobs_o, 0)
+    o_s[y, c, x] = unpack_o(whole_of(z_s, 48, 64))
+    q_s[y, c, x] = unpack_q(whole_of(z_s, 0, 48))
+    each(open_second, jobs_o)
+    each(pass_on, jobs_q, 0)
+    each(first_step, jobs_s, 0)
+    send_mid(28, 46)
+    each(open_second, jobs_q)
+    each(on_second, jobs_o)
+    send_mid(46, 63)
+    each(pass_on, jobs_s, 0)
     each(end_second, jobs_o)
 
     each(share_wait, jobs_o)
@@ -369,16 +365,10 @@
     for b in range(2):
         part = dot(back[128 * b:128 * b + 128, :], dout[...])
         dsend[b] = part.astype(bf16).reshape(NSEQ, 2, HEADS * HP)
-        scatter(dsend.at[b], drecv.at[b], 1 + b)
-        drecv[b, s] = dsend[b, s]
+    each_peer(lambda to: send_pair(dsend, drecv, 1, to))
+    drecv[:, s] = dsend[:, s]
     mrecv[s] = msend[s]
-    each(pass_on, jobs_q, 0)
-    ring_step(1, 8)
-    o_s[y, c, x] = unpack_o(whole_of(z_s, 48, 64))
-    q_s[y, c, x] = unpack_q(whole_of(z_s, 0, 48))
-    each(open_second, jobs_q)
-    each(first_step, jobs_s, 0)
-    lax.fori_loop(0, 4, own_norms, 0)
+    each(open_second, jobs_s)
     each(on_second, jobs_q)
     each(end_second, jobs_q)
 
@@ -442,18 +432,16 @@
         normin[rows, :] = (normed * (1.0 + mod[4]) + mod[3]).astype(bf16)
         return carry
     lax.fori_loop(0, 4, patch_norm, 0)
-    each(pass_on, jobs_s, 0)
-    each(open_second, jobs_s)
     each(share_wait, jobs_q)
+    project(q_t, 0, TOK)
+    attend(True)
+    wait_pairs(drecv, arecv_sem, 1)
+    dout[...] = drecv[...].reshape(TOK, HEADS * HP)
     for b in range(2):
-        project(q_t, 128 * b, 128)
-        attend(True, b, b + 1)
-        wait_scatter(drecv.at[b], arecv_sem, 1 + b)
-        dout[128 * b:128 * b + 128, :] = drecv[b].reshape(128, HEADS * HP)
         attend_back(b, b + 1)
         project_back(q_t, 128 * b, 128)
         rsend[b] = acc[128 * b:128 * b + 128, :].astype(bf16).reshape(NSEQ, 2, D)
-        scatter(rsend.at[b], rrecv.at[b], 3 + b)
+        scatter(rsend.at[b], rrecv.at[b], 2 + b)
         rrecv[b, s] = rsend[b, s]
         if b == 0:
             each(on_second, jobs_s)
@@ -471,14 +459,12 @@
 
     for cp in pending:
         cp.wait_send()
-    o_wait(0)
     wait_scatter(msend, asend_sem, 0)
-    for b in range(2):
-        wait_scatter(dsend.at[b], asend_sem, 1 + b)
-
-    wait_scatter(rrecv.at[0], arecv_sem, 3)
+    wait_pairs(dsend, asend_sem, 1)
+
+    wait_scatter(rrecv.at[0], arecv_sem, 2)
     acc[...] = dot(back[:, 0:128], rrecv[0].reshape(128, D))
-    wait_scatter(rrecv.at[1], arecv_sem, 4)
+    wait_scatter(rrecv.at[1], arecv_sem, 3)
     acc[...] += dot(back[:, 128:256], rrecv[1].reshape(128, D))
 
     def mid_grad(i, carry):
@@ -505,7 +491,7 @@
     lax.fori_loop(0, 4, last_grad, 0)
 
     for b in range(2):
-        wait_scatter(rsend.at[b], asend_sem, 3 + b)
+        wait_scatter(rsend.at[b], asend_sem, 2 + b)
 
 
 def per_device(inputs, mid_inputs, cotangent, modulation, frames, qkv_s, out_s, qkv_t, out_t):
@@ -526,9 +512,8 @@
             pltpu.VMEM((27, 144), bf16),
             pltpu.VMEM((18, 72), bf16),
             dma((8,)),
-            pltpu.VMEM((NZ, 48, 128), bf16),
             pltpu.VMEM((NZ, 64, 128), bf16),
-            pltpu.VMEM((NZ, 16, 128), bf16),
+            pltpu.VMEM((NZ, 64, 128), bf16),
             pltpu.VMEM((NZ, 128, QW), bf16),
             pltpu.VMEM((NZ, 128, OW), bf16),
             pltpu.VMEM((NY, 2, NX, 144, QW), bf16),
@@ -555,7 +540,7 @@
             pltpu.VMEM((TOK, D), f32),
             pltpu.VMEM((TOK, 1), f32),
             pltpu.VMEM((TOK, D), f32),
-            dma((2,)), dma((2, 2, 8)), dma((2, 2, 8)), dma((8, 12)), dma((8, 12)), dma((5,)), dma((5,)),
+            dma((2, 2, 8)), dma((2, 2, 8)), dma((4, 12)), dma((4, 12)), dma((4,)), dma((4,)),
         ],
         compiler_params=pltpu.CompilerParams(
             collective_id=0, has_side_effects=True, vmem_limit_bytes=56 * 1024 * 1024

time: 130 us -> 142 us (1.092)
  Pallas kernels: 127 us -> 139 us
    pallas_call x1, Pallas kernels: 127 us -> 139 us  [per_device(): pl.pallas_call(kernel, out_shape=jax.ShapeDtypeStruct((2, 128, D), bf16),...]
where the time goes in v9:
time: 142 us; the launch traced here: 141 us
  Pallas kernels  139 us (98%)
  local copies, waits for them, and re-layouts  1.92 us (1%)
    pallas_call x1, Pallas kernels, per_device(): pl.pallas_call(kernel, out_shape=jax.ShapeDtypeStruct((2, 128, D), bf16),...  139 us

profile of v9, /device:TPU:1, one launch (start us, length us, event | category | flops | bytes accessed | tf_op | source)
XLA Modules:
  0.0 141.3 jit_solution(15436078912852031752)
XLA Ops:
  0.7 138.8 %blocks_grad.1 = bf16[2,128,1152]{2,1,0:T(8,128)(2,1)} custom-call(bf16[2,128,1152]{2,1,0:T(8,128)(2,1)} %bitcast.10, bf16[2,128,1152]{2,1,0:T(8,128)(2,1)} %bitcast.11, bf16[2,128,1152]{2,1,0:T(8,128)(2,1)} %bitcast.12, f32[6,1,1152]{2,1,0:T(1,128)} %bitcast.13, s32[1]{0:T(128)S(6)} %copy.11.frames, bf16[27,144]{1,0:T(8,128)(2,1)} %bitcast.14, ...), custom_call_target="tpu_custom_call" | custom-call | tf_op jit(solution)/shard_map/blocks_grad/pallas_call | solution.py:500
  139.4 1.9 %copy.12 = bf16[1,2,128,1152]{3,2,1,0:T(8,128)(2,1)} copy(bf16[1,2,128,1152]{3,2,1,0:T(8,128)(2,1)} %bitcast.9) | data formatting | bytes 1179648

commit v10 on v9

--- a/solution.py
+++ b/solution.py
@@ -154,17 +154,6 @@
             device_id={"seq": to},
         ).start()
 
-    def send_pair(src, dst, k, to):
-        pltpu.make_async_remote_copy(
-            src_ref=src.at[:, to], dst_ref=dst.at[:, s],
-            send_sem=asend_sem.at[k], recv_sem=arecv_sem.at[k],
-            device_id={"seq": to},
-        ).start()
-
-    def wait_pairs(ref, sem, k):
-        part = ref.at[:, pl.ds(0, NSEQ - 1)]
-        pltpu.make_async_copy(part, part, sem.at[k]).wait()
-
     def scatter(src, dst, k):
         each_peer(lambda to: send_to(src, dst, k, to))
 
@@ -223,9 +212,12 @@
     def unpack_o(whole):
         return unpack(whole, eo, 16, 24, 5)
 
-    jobs_o = [(0, o_t, "y", 0, 80, 48)]
-    jobs_q = [(1, q_t, "x", 0, 144, 80)]
-    jobs_s = [(2, o_s, "x", 0, 80, 48), (3, q_s, "y", 0, 144, 80)]
+    jobs_o = [(0, o_t, "y", 0, 48, 32), (1, o_t, "x", 48, 32, 16)]
+    jobs_q = [(2, q_t, "y", 0, 112, 64), (3, q_t, "x", 112, 32, 16)]
+    jobs_s = [
+        (4, o_s, "y", 0, 48, 32), (5, o_s, "x", 48, 32, 16),
+        (6, q_s, "y", 0, 112, 64), (7, q_s, "x", 112, 32, 16),
+    ]
 
     def view(job, phase, rel, half, core):
         _, ref, first, r, n, m = job
@@ -329,7 +321,7 @@
         if step > 0:
             ring_step(0, step)
             ring_step(1, step)
-        send_mid(2 * step, 2 * step + 2)
+        send_mid(step, step + 1)
         lax.fori_loop(2 * step, 2 * step + 2, fill_o, 0)
         lax.fori_loop(2 * step, 2 * step + 2, fill_q, 0)
         if step == 1:
@@ -345,30 +337,29 @@
     each(first_step, jobs_o, 0)
     q_t[y, c, x] = unpack_q(whole_of(z_t, 0, 48))
     each(first_step, jobs_q, 0)
-    send_mid(16, 28)
+    send_mid(8, 20)
     ring_step(1, 8)
-    each(pass_on, jobs_o, 0)
     o_s[y, c, x] = unpack_o(whole_of(z_s, 48, 64))
     q_s[y, c, x] = unpack_q(whole_of(z_s, 0, 48))
+    each(pass_on, jobs_o, 0)
     each(open_second, jobs_o)
+    send_mid(20, 32)
     each(pass_on, jobs_q, 0)
+    send_mid(32, 44)
+    each(on_second, jobs_o)
+    each(open_second, jobs_q)
+    send_mid(44, 63)
+    each(end_second, jobs_o)
     each(first_step, jobs_s, 0)
-    send_mid(28, 46)
-    each(open_second, jobs_q)
-    each(on_second, jobs_o)
-    send_mid(46, 63)
-    each(pass_on, jobs_s, 0)
-    each(end_second, jobs_o)
 
     each(share_wait, jobs_o)
     dout[...] = out_back(normin, o_t)
     for b in range(2):
         part = dot(back[128 * b:128 * b + 128, :], dout[...])
         dsend[b] = part.astype(bf16).reshape(NSEQ, 2, HEADS * HP)
-    each_peer(lambda to: send_pair(dsend, drecv, 1, to))
-    drecv[:, s] = dsend[:, s]
+        scatter(dsend.at[b], drecv.at[b], 1 + b)
+        drecv[b, s] = dsend[b, s]
     mrecv[s] = msend[s]
-    each(open_second, jobs_s)
     each(on_second, jobs_q)
     each(end_second, jobs_q)
 
@@ -432,16 +423,18 @@
         normin[rows, :] = (normed * (1.0 + mod[4]) + mod[3]).astype(bf16)
         return carry
     lax.fori_loop(0, 4, patch_norm, 0)
+    each(pass_on, jobs_s, 0)
+    each(open_second, jobs_s)
     each(share_wait, jobs_q)
-    project(q_t, 0, TOK)
-    attend(True)
-    wait_pairs(drecv, arecv_sem, 1)
-    dout[...] = drecv[...].reshape(TOK, HEADS * HP)
     for b in range(2):
+        project(q_t, 128 * b, 128)
+        attend(True, b, b + 1)
+        wait_scatter(drecv.at[b], arecv_sem, 1 + b)
+        dout[128 * b:128 * b + 128, :] = drecv[b].reshape(128, HEADS * HP)
         attend_back(b, b + 1)
         project_back(q_t, 128 * b, 128)
         rsend[b] = acc[128 * b:128 * b + 128, :].astype(bf16).reshape(NSEQ, 2, D)
-        scatter(rsend.at[b], rrecv.at[b], 2 + b)
+        scatter(rsend.at[b], rrecv.at[b], 3 + b)
         rrecv[b, s] = rsend[b, s]
         if b == 0:
             each(on_second, jobs_s)
@@ -460,11 +453,12 @@
     for cp in pending:
         cp.wait_send()
     wait_scatter(msend, asend_sem, 0)
-    wait_pairs(dsend, asend_sem, 1)
-
-    wait_scatter(rrecv.at[0], arecv_sem, 2)
+    for b in range(2):
+        wait_scatter(dsend.at[b], asend_sem, 1 + b)
+
+    wait_scatter(rrecv.at[0], arecv_sem, 3)
     acc[...] = dot(back[:, 0:128], rrecv[0].reshape(128, D))
-    wait_scatter(rrecv.at[1], arecv_sem, 3)
+    wait_scatter(rrecv.at[1], arecv_sem, 4)
     acc[...] += dot(back[:, 128:256], rrecv[1].reshape(128, D))
 
     def mid_grad(i, carry):
@@ -491,7 +485,7 @@
     lax.fori_loop(0, 4, last_grad, 0)
 
     for b in range(2):
-        wait_scatter(rsend.at[b], asend_sem, 2 + b)
+        wait_scatter(rsend.at[b], asend_sem, 3 + b)
 
 
 def per_device(inputs, mid_inputs, cotangent, modulation, frames, qkv_s, out_s, qkv_t, out_t):
@@ -540,7 +534,7 @@
             pltpu.VMEM((TOK, D), f32),
             pltpu.VMEM((TOK, 1), f32),
             pltpu.VMEM((TOK, D), f32),
-            dma((2, 2, 8)), dma((2, 2, 8)), dma((4, 12)), dma((4, 12)), dma((4,)), dma((4,)),
+            dma((2, 2, 8)), dma((2, 2, 8)), dma((8, 12)), dma((8, 12)), dma((5,)), dma((5,)),
         ],
         compiler_params=pltpu.CompilerParams(
             collective_id=0, has_side_effects=True, vmem_limit_bytes=56 * 1024 * 1024

time: 142 us -> 128 us (0.901)
  Pallas kernels: 139 us -> 125 us
    pallas_call x1, Pallas kernels: 139 us -> 125 us  [per_device(): pl.pallas_call(kernel, out_shape=jax.ShapeDtypeStruct((2, 128, D), bf16),...]
where the time goes in v10:
time: 128 us
  Pallas kernels  125 us (98%)
  local copies, waits for them, and re-layouts  1.92 us (2%)
    pallas_call x1, Pallas kernels, per_device(): pl.pallas_call(kernel, out_shape=jax.ShapeDtypeStruct((2, 128, D), bf16),...  125 us

profile of v10, /device:TPU:1, one launch (start us, length us, event | category | flops | bytes accessed | tf_op | source)
XLA Modules:
  0.0 127.5 jit_solution(16425008576219059609)
XLA Ops:
  0.7 125.0 %blocks_grad.1 = bf16[2,128,1152]{2,1,0:T(8,128)(2,1)} custom-call(bf16[2,128,1152]{2,1,0:T(8,128)(2,1)} %bitcast.10, bf16[2,128,1152]{2,1,0:T(8,128)(2,1)} %bitcast.11, bf16[2,128,1152]{2,1,0:T(8,128)(2,1)} %bitcast.12, f32[6,1,1152]{2,1,0:T(1,128)} %bitcast.13, s32[1]{0:T(128)S(6)} %copy.11.frames, bf16[27,144]{1,0:T(8,128)(2,1)} %bitcast.14, ...), custom_call_target="tpu_custom_call" | custom-call | tf_op jit(solution)/shard_map/blocks_grad/pallas_call | solution.py:494
  125.6 1.9 %copy.12 = bf16[1,2,128,1152]{3,2,1,0:T(8,128)(2,1)} copy(bf16[1,2,128,1152]{3,2,1,0:T(8,128)(2,1)} %bitcast.9) | data formatting | bytes 1179648

commit v11 on v10

--- a/solution.py
+++ b/solution.py
@@ -359,8 +359,9 @@
         dsend[b] = part.astype(bf16).reshape(NSEQ, 2, HEADS * HP)
         scatter(dsend.at[b], drecv.at[b], 1 + b)
         drecv[b, s] = dsend[b, s]
+        if b == 0:
+            each(on_second, jobs_q)
     mrecv[s] = msend[s]
-    each(on_second, jobs_q)
     each(end_second, jobs_q)
 
     def project(q_ref, lo, n):
@@ -429,6 +430,8 @@
     for b in range(2):
         project(q_t, 128 * b, 128)
         attend(True, b, b + 1)
+        if b == 1:
+            each(on_second, jobs_s)
         wait_scatter(drecv.at[b], arecv_sem, 1 + b)
         dout[128 * b:128 * b + 128, :] = drecv[b].reshape(128, HEADS * HP)
         attend_back(b, b + 1)
@@ -436,8 +439,6 @@
         rsend[b] = acc[128 * b:128 * b + 128, :].astype(bf16).reshape(NSEQ, 2, D)
         scatter(rsend.at[b], rrecv.at[b], 3 + b)
         rrecv[b, s] = rsend[b, s]
-        if b == 0:
-            each(on_second, jobs_s)
 
     each(end_second, jobs_s)
 

time: 128 us -> 127 us (level)
    pallas_call x1, Pallas kernels: 125 us -> 124 us  [per_device(): pl.pallas_call(kernel, out_shape=jax.ShapeDtypeStruct((2, 128, D), bf16),...]
where the time goes in v11:
time: 127 us; the launch traced here: 126 us
  Pallas kernels  124 us (98%)
  local copies, waits for them, and re-layouts  1.92 us (2%)
    pallas_call x1, Pallas kernels, per_device(): pl.pallas_call(kernel, out_shape=jax.ShapeDtypeStruct((2, 128, D), bf16),...  124 us

profile of v11, /device:TPU:1, one launch (start us, length us, event | category | flops | bytes accessed | tf_op | source)
XLA Modules:
  0.0 126.1 jit_solution(17795102061730639575)
XLA Ops:
  0.7 123.6 %blocks_grad.1 = bf16[2,128,1152]{2,1,0:T(8,128)(2,1)} custom-call(bf16[2,128,1152]{2,1,0:T(8,128)(2,1)} %bitcast.10, bf16[2,128,1152]{2,1,0:T(8,128)(2,1)} %bitcast.11, bf16[2,128,1152]{2,1,0:T(8,128)(2,1)} %bitcast.12, f32[6,1,1152]{2,1,0:T(1,128)} %bitcast.13, s32[1]{0:T(128)S(6)} %copy.11.frames, bf16[27,144]{1,0:T(8,128)(2,1)} %bitcast.14, ...), custom_call_target="tpu_custom_call" | custom-call | tf_op jit(solution)/shard_map/blocks_grad/pallas_call | solution.py:495
  124.2 1.9 %copy.12 = bf16[1,2,128,1152]{3,2,1,0:T(8,128)(2,1)} copy(bf16[1,2,128,1152]{3,2,1,0:T(8,128)(2,1)} %bitcast.9) | data formatting | bytes 1179648

commit v12 on v11

--- a/solution.py
+++ b/solution.py
@@ -372,13 +372,13 @@
         lax.fori_loop(0, NY, body, 0)
 
     def project_back(q_ref, lo, n):
-        acc[lo:lo + n, :] = jnp.zeros((n, D), f32)
-
-        def body(yy, carry):
-            lanes = pl.ds(pl.multiple_of(yy * QW, QW), QW)
-            acc[lo:lo + n, :] += dot(dqkv[lo:lo + n, lanes], qkv_rows(q_ref, yy), NT)
-            return carry
-        lax.fori_loop(0, NY, body, 0)
+        for at in range(0, D, 384):
+            total = None
+            for yy in range(NY):
+                part = dqkv[lo:lo + n, yy * QW:(yy + 1) * QW]
+                term = dot(part, qkv_rows(q_ref, yy)[at:at + 384], NT)
+                total = term if total is None else total + term
+            acc[lo:lo + n, at:at + 384] = total
 
     def attend(masked, lo=0, hi=2):
         def body(b, carry):

time: 127 us -> 126 us (level)
  Pallas kernels: 124 us -> 122 us
where the time goes in v12:
time: 126 us; the launch traced here: 125 us
  Pallas kernels  122 us (97%)
  local copies, waits for them, and re-layouts  1.92 us (2%)
    pallas_call x1, Pallas kernels, per_device(): pl.pallas_call(kernel, out_shape=jax.ShapeDtypeStruct((2, 128, D), bf16),...  122 us

profile of v12, /device:TPU:1, one launch (start us, length us, event | category | flops | bytes accessed | tf_op | source)
XLA Modules:
  0.0 125.1 jit_solution(2755349924072996111)
XLA Ops:
  0.7 122.5 %blocks_grad.1 = bf16[2,128,1152]{2,1,0:T(8,128)(2,1)} custom-call(bf16[2,128,1152]{2,1,0:T(8,128)(2,1)} %bitcast.10, bf16[2,128,1152]{2,1,0:T(8,128)(2,1)} %bitcast.11, bf16[2,128,1152]{2,1,0:T(8,128)(2,1)} %bitcast.12, f32[6,1,1152]{2,1,0:T(1,128)} %bitcast.13, s32[1]{0:T(128)S(6)} %copy.11.frames, bf16[27,144]{1,0:T(8,128)(2,1)} %bitcast.14, ...), custom_call_target="tpu_custom_call" | custom-call | tf_op jit(solution)/shard_map/blocks_grad/pallas_call | solution.py:495
  123.1 1.9 %copy.12 = bf16[1,2,128,1152]{3,2,1,0:T(8,128)(2,1)} copy(bf16[1,2,128,1152]{3,2,1,0:T(8,128)(2,1)} %bitcast.9) | data formatting | bytes 1179648
